TPU v7x, 32 devices: a whole 2x2x4 slice. The times are simulated.
32 devices in a mesh: grp: 8 (over y, x, core), shard: 4 (over z).
Axes of the slice: x: 2, y: 2, z: 4, core: 2. Of those that a mesh axis runs over, the one named last changes fastest.
Arguments:
- x_in: bfloat16 [7168, 2048], P(('grp', 'shard')), may hold values from -6 to 6
- d_out: bfloat16 [7168, 2048], P(('grp', 'shard')), may hold values from -6 to 6
- w_qkv: bfloat16 [2048, 6144], P(('grp', 'shard')), may hold values from -0.125 to 0.125
- w_dense: bfloat16 [2048, 2048], P(('grp', 'shard')), may hold values from -6 to 6
- w_in: bfloat16 [2048, 10922], P(('grp', 'shard')), may hold values from -0.125 to 0.125
- w_out: bfloat16 [2048, 5461], P(('grp', 'shard')), may hold values from -1 to 1
- gain_one: bfloat16 [2048], P(('grp', 'shard')), may hold values from 0.5 to 1.5
- bias_one: bfloat16 [2048], P(('grp', 'shard')), may hold values from -1 to 1
- gain_two: bfloat16 [2048], P(('grp', 'shard')), may hold values from 0.5 to 1.5
- bias_two: bfloat16 [2048], P(('grp', 'shard')), may hold values from -1 to 1
- mlm_flags: int32 [7168], P(('grp', 'shard')), may hold values from 0 to 1, as said below
- span_start: int32 [32], P(('grp', 'shard')), may hold values from 0 to 111, as said below
- span_len: int32 [32], P(('grp', 'shard')), may hold values from 28 to 112, as said below
Outputs:
- layer_out: bfloat16 [7168, 2048], P(('grp', 'shard'))
- d_input: bfloat16 [7168, 2048], P(('grp', 'shard'))
- d_w_qkv: float32 [2048, 6144], P(('grp', 'shard'))
- d_w_dense: float32 [2048, 2048], P(('grp', 'shard'))
- d_w_in: float32 [2048, 10922], P(('grp', 'shard'))
- d_w_out: float32 [2048, 5461], P(('grp', 'shard'))
- d_gain_one: float32 [2048], P(('grp', 'shard'))
- d_bias_one: float32 [2048], P(('grp', 'shard'))
- d_gain_two: float32 [2048], P(('grp', 'shard'))
- d_bias_two: float32 [2048], P(('grp', 'shard'))
Inputs may be any that keep to these rules, and one draw needn't show every extreme that they name: `mlm_flags`: flags are 1 only in max(1, 6) sequences, the MLM ones, and there the first token's flag is always 1. `span_len`: the most is reached in every draw. `span_start`: below the sequence's prefix; the most is reached in every draw.
All inputs are finite; a program needn't handle non-finite values.
Results may differ from a plain program's by a relative error of at most 0.02.
Values may be sent and summed in bfloat16 or wider, within the bound.
A program may use at most 512 MiB of HBM per device.

v0:
```python
import functools

import jax
import jax.numpy as jnp
from jax import lax
from jax.experimental import pallas as pl
from jax.experimental.pallas import tpu as pltpu
from jax.sharding import Mesh
from jax.sharding import PartitionSpec as P

HEADS = 16
HEAD = 128
SEQ_LEN = 224
D = HEADS * HEAD
deep_alpha = 6.928203230275509
norm_eps = 1e-05
far_below = -1e30
scale = HEAD ** (-0.5)

ALL = ("gy", "gx", "core", "z")
GROUP = ("gy", "gx", "core")
MESH = pl.DeviceIdType.MESH
F32 = jnp.float32
BF16 = jnp.bfloat16


def dot(left, right):
    return jnp.dot(left, right, preferred_element_type=F32)


def dot_rows(left, right):
    return lax.dot_general(left, right, (((0,), (0,)), ((), ())), preferred_element_type=F32)


def dot_cols(left, right):
    return lax.dot_general(left, right, (((1,), (1,)), ((), ())), preferred_element_type=F32)


def swap_halves(block):
    lane = lax.broadcasted_iota(jnp.int32, block.shape, 1)
    return jnp.where((lane & 32) == 0, pltpu.roll(block, 96, 1), pltpu.roll(block, 32, 1))


def seen(prefix):
    row = lax.broadcasted_iota(jnp.int32, (SEQ_LEN, SEQ_LEN), 0)
    col = lax.broadcasted_iota(jnp.int32, (SEQ_LEN, SEQ_LEN), 1)
    return (col < prefix) | (col <= row)


def softmax(queries, keys, visible):
    scores = jnp.where(visible, dot_cols(queries, keys), far_below)
    weights = jnp.exp(scores - jnp.max(scores, axis=1, keepdims=True))
    return weights / jnp.sum(weights, axis=1, keepdims=True)


def attend_kernel(prefix_ref, packed_ref, cos_ref, sin_ref, qkv_ref, context_ref):
    width = context_ref.shape[1]
    visible = seen(prefix_ref[pl.program_id(0)])
    cosine = cos_ref[0]
    sine = sin_ref[0]
    for head in range(width // HEAD):
        at = pl.ds(head * HEAD, HEAD)
        at_k = pl.ds(width + head * HEAD, HEAD)
        at_v = pl.ds(2 * width + head * HEAD, HEAD)
        raw = packed_ref[:, at]
        queries = ((raw * cosine + swap_halves(raw) * sine) * scale).astype(BF16)
        raw = packed_ref[:, at_k]
        keys = (raw * cosine + swap_halves(raw) * sine).astype(BF16)
        values = packed_ref[:, at_v].astype(BF16)
        qkv_ref[:, at] = queries
        qkv_ref[:, at_k] = keys
        qkv_ref[:, at_v] = values
        probs = softmax(queries, keys, visible).astype(BF16)
        context_ref[:, at] = dot(probs, values).astype(BF16)


def attend_back_kernel(prefix_ref, qkv_ref, d_context_ref, cos_ref, sin_ref, d_packed_ref):
    width = d_context_ref.shape[1]
    visible = seen(prefix_ref[pl.program_id(0)])
    cosine = cos_ref[0]
    sine = sin_ref[0]
    for head in range(width // HEAD):
        at = pl.ds(head * HEAD, HEAD)
        at_k = pl.ds(width + head * HEAD, HEAD)
        at_v = pl.ds(2 * width + head * HEAD, HEAD)
        queries = qkv_ref[:, at]
        keys = qkv_ref[:, at_k]
        values = qkv_ref[:, at_v]
        d_context = d_context_ref[:, at]
        probs = softmax(queries, keys, visible)
        d_packed_ref[:, at_v] = dot_rows(probs.astype(BF16), d_context).astype(BF16)
        d_probs = dot_cols(d_context, values)
        inner = jnp.sum(probs * d_probs, axis=1, keepdims=True)
        d_scores = (probs * (d_probs - inner)).astype(BF16)
        grad = dot(d_scores, keys) * scale
        d_packed_ref[:, at] = (grad * cosine - swap_halves(grad) * sine).astype(BF16)
        grad = dot_rows(d_scores, queries)
        d_packed_ref[:, at_k] = (grad * cosine - swap_halves(grad) * sine).astype(BF16)


def by_sequence(width):
    return pl.BlockSpec((SEQ_LEN, width), lambda s: (s, 0))


TABLE = pl.BlockSpec((1, SEQ_LEN, HEAD), lambda s: (s, 0, 0))
SCALARS = pl.BlockSpec(memory_space=pltpu.SMEM)
PARAMS = pltpu.CompilerParams(vmem_limit_bytes=56 * 2**20)


def attend(prefix, packed, cosine, sine):
    rows, width = packed.shape[0], packed.shape[1] // 3
    return pl.pallas_call(
        attend_kernel,
        grid=(rows // SEQ_LEN,),
        in_specs=[SCALARS, by_sequence(3 * width), TABLE, TABLE],
        out_specs=[by_sequence(3 * width), by_sequence(width)],
        out_shape=[
            jax.ShapeDtypeStruct((rows, 3 * width), BF16),
            jax.ShapeDtypeStruct((rows, width), BF16),
        ],
        compiler_params=PARAMS,
    )(prefix, packed, cosine, sine)


def attend_back(prefix, qkv, d_context, cosine, sine):
    rows, width = d_context.shape
    return pl.pallas_call(
        attend_back_kernel,
        grid=(rows // SEQ_LEN,),
        in_specs=[SCALARS, by_sequence(3 * width), by_sequence(width), TABLE, TABLE],
        out_specs=by_sequence(3 * width),
        out_shape=jax.ShapeDtypeStruct((rows, 3 * width), BF16),
        compiler_params=PARAMS,
    )(prefix, qkv, d_context, cosine, sine)


def tables(prefix, start):
    place = jnp.arange(SEQ_LEN, dtype=jnp.int32)
    in_span = place[None, :] >= prefix[:, None]
    pos_one = jnp.where(in_span, start[:, None], place[None, :])
    pos_two = jnp.where(in_span, place[None, :] - prefix[:, None] + 1, 0)
    lane = jnp.arange(HEAD)
    freqs = 10000.0 ** (-2.0 * (lane % 32).astype(F32) / 64)
    place_of = jnp.where(lane[None, None, :] < 64, pos_one[:, :, None], pos_two[:, :, None])
    angles = place_of.astype(F32) * freqs
    sign = jnp.where(lane % 64 < 32, -1.0, 1.0)
    return jnp.cos(angles), jnp.sin(angles) * sign


def norm_parts(values):
    center = values - jnp.mean(values, axis=-1, keepdims=True)
    inverse = lax.rsqrt(jnp.mean(center * center, axis=-1, keepdims=True) + norm_eps)
    return center * inverse, inverse


def norm_back(normal, inverse, gain, grad):
    scaled = gain * grad
    return inverse * (
        scaled
        - jnp.mean(scaled, axis=-1, keepdims=True)
        - normal * jnp.mean(scaled * normal, axis=-1, keepdims=True)
    )


def gate_parts(gate):
    phi = 0.5 * (1.0 + lax.erf(gate * 0.7071067811865476))
    slope = phi + gate * jnp.exp(-0.5 * gate * gate) * 0.3989422804014327
    return gate * phi, slope


def here():
    return lax.axis_index("gy"), lax.axis_index("gx"), lax.axis_index("core")


def place(y, x, c):
    return (y * 2 + x) * 2 + c


def greet(peers):
    barrier = pltpu.get_barrier_semaphore()
    for peer in peers:
        pl.semaphore_signal(barrier, inc=1, device_id=peer, device_id_type=MESH)
    pl.semaphore_wait(barrier, len(peers))


def spread_block(cut, base, block_ref, out_ref, send, recv, local):
    rows = block_ref.shape[0]
    y, x, c = here()
    to_x, to_y, to_c = {"gx": 1 - x}, {"gy": 1 - y}, {"core": 1 - c}
    me, by_x, by_y, far = place(y, x, c), place(y, 1 - x, c), place(1 - y, x, c), place(1 - y, 1 - x, c)
    low, high = pl.ds(0, cut), pl.ds(cut, rows - cut)

    def push(k, src, dst, to):
        copy = pltpu.make_async_remote_copy(
            src_ref=src, dst_ref=dst, send_sem=send.at[base + k], recv_sem=recv.at[base + k], device_id=to, device_id_type=MESH
        )
        copy.start()
        return copy

    def landed(k, dst):
        pltpu.make_async_remote_copy(
            src_ref=dst, dst_ref=dst, send_sem=send.at[base + k], recv_sem=recv.at[base + k], device_id=to_c, device_id_type=MESH
        ).wait_recv()

    sent = [
        push(0, block_ref.at[low], out_ref.at[me, low], to_x),
        push(1, block_ref.at[high], out_ref.at[me, high], to_y),
        push(2, block_ref.at[high], out_ref.at[me, high], to_x),
        push(3, block_ref.at[low], out_ref.at[me, low], to_y),
        push(4, block_ref, out_ref.at[me], to_c),
    ]
    keep = pltpu.make_async_copy(block_ref, out_ref.at[me], local)
    keep.start()
    landed(0, out_ref.at[by_x, low])
    sent.append(push(5, out_ref.at[by_x, low], out_ref.at[by_x, low], to_y))
    sent.append(push(7, out_ref.at[by_x, low], out_ref.at[by_x, low], to_c))
    landed(1, out_ref.at[by_y, high])
    sent.append(push(6, out_ref.at[by_y, high], out_ref.at[by_y, high], to_x))
    sent.append(push(8, out_ref.at[by_y, high], out_ref.at[by_y, high], to_c))
    landed(2, out_ref.at[by_x, high])
    sent.append(push(9, out_ref.at[by_x, high], out_ref.at[by_x, high], to_c))
    landed(3, out_ref.at[by_y, low])
    sent.append(push(10, out_ref.at[by_y, low], out_ref.at[by_y, low], to_c))
    landed(5, out_ref.at[far, low])
    sent.append(push(11, out_ref.at[far, low], out_ref.at[far, low], to_c))
    landed(6, out_ref.at[far, high])
    sent.append(push(12, out_ref.at[far, high], out_ref.at[far, high], to_c))
    other, other_x, other_y, other_far = (
        place(y, x, 1 - c),
        place(y, 1 - x, 1 - c),
        place(1 - y, x, 1 - c),
        place(1 - y, 1 - x, 1 - c),
    )
    landed(4, out_ref.at[other])
    landed(7, out_ref.at[other_x, low])
    landed(8, out_ref.at[other_y, high])
    landed(9, out_ref.at[other_x, high])
    landed(10, out_ref.at[other_y, low])
    landed(11, out_ref.at[other_far, low])
    landed(12, out_ref.at[other_far, high])
    keep.wait()
    for copy in sent:
        copy.wait_send()


ANY = pl.BlockSpec(memory_space=pl.ANY)


def swap_peers(zs, kinds):
    y, x, c = here()
    z = lax.axis_index("z")
    found = []
    for k in range(1, 8):
        peer = ((y + k // 4) % 2, (x + k // 2 % 2) % 2, (c + k % 2) % 2)
        found.append((place(*peer), {"gy": peer[0], "gx": peer[1], "core": peer[2]}))
    if "line" in kinds:
        found += [((z + k) % zs, {"z": (z + k) % zs}) for k in range(1, zs)]
    return found


def swap_begin(zs, kinds, blocks, outs, send, recv, local):
    copies, comes, keeps = [], [], []
    found = swap_peers(zs, kinds)
    for i, kind in enumerate(kinds):
        me = lax.axis_index("z") if kind == "line" else place(*here())
        for k, (peer, name) in enumerate(found[7:] if kind == "line" else found[:7]):
            src = blocks[i].at[peer] if kind == "swap" else blocks[i]
            landing = outs[i].at[peer]
            sems = dict(send_sem=send.at[i, k], recv_sem=recv.at[i, k], device_id=name, device_id_type=MESH)
            copies.append(pltpu.make_async_remote_copy(src_ref=src, dst_ref=outs[i].at[me], **sems))
            comes.append(pltpu.make_async_remote_copy(src_ref=landing, dst_ref=landing, **sems))
            copies[-1].start()
        own = blocks[i].at[me] if kind == "swap" else blocks[i]
        keeps.append(pltpu.make_async_copy(own, outs[i].at[me], local.at[i]))
        keeps[-1].start()

    def finish():
        for come in comes:
            come.wait_recv()
        for copy in copies:
            copy.wait_send()
        for keep in keeps:
            keep.wait()

    return finish


SWAP_LEAD = {"swap": lambda zs: (), "group": lambda zs: (8,), "line": lambda zs: (zs,)}


def swap_shapes(zs, arrays, kinds):
    return [jax.ShapeDtypeStruct(SWAP_LEAD[k](zs) + a.shape, a.dtype) for a, k in zip(arrays, kinds)]


def swap_scratch(zs, kinds):
    n, most = len(kinds), max(7, zs - 1)
    return [
        pltpu.SemaphoreType.DMA((n, most)),
        pltpu.SemaphoreType.DMA((n, most)),
        pltpu.SemaphoreType.DMA((n,)),
    ]


SLAB = 16
ROWS = pl.BlockSpec(memory_space=pltpu.VMEM)
CHIP_COLS = 256


def by_rows(value, zs, piece):
    group = D // (zs * piece)
    order = [g * zs + z for z in range(zs) for g in range(group)]
    return jnp.concatenate([value[:, m * piece : (m + 1) * piece] for m in order], axis=1)


def in_order(value, zs, piece):
    group = D // (zs * piece)
    order = [z * group + g for g in range(group) for z in range(zs)]
    return jnp.concatenate([value[:, m * piece : (m + 1) * piece] for m in order], axis=1)


def first_norm(values, gains):
    normal, inverse = norm_parts(values)
    first = normal * gains[0:1] + gains[1:2]
    return first, normal, inverse


def second_norm(total, first, grad, gains):
    normal, inverse = norm_parts(deep_alpha * first + total)
    return normal * gains[2:3] + gains[3:4], norm_back(normal, inverse, gains[2:3], grad), grad * normal


def first_back(total, d_pre_two, normal, inverse, gains):
    d_first = deep_alpha * d_pre_two + total
    return norm_back(normal, inverse, gains[0:1], d_first), d_first * normal, d_first


def fold_kernel(mode, across, zs, piece, n_aux, n_out, kinds, *refs):
    left_ref, right_ref, gains_ref = refs[:3]
    aux_refs = refs[3 : 3 + n_aux]
    refs = refs[3 + n_aux :]
    n_swap = len(kinds)
    swap_in, refs = refs[:n_swap], refs[n_swap:]
    spread = mode != "last"
    if spread:
        all_ref, refs = refs[0], refs[1:]
    outs, refs = refs[:n_out], refs[n_out:]
    swap_out, refs = refs[:n_swap], refs[n_swap:]
    aux, refs = refs[:n_aux], refs[n_aux:]
    left, right, part, got, near_x, near_y, from_x, from_y, block, acc, send, recv, local = refs[:13]
    rows, width = block.shape
    cut = near_x.shape[0]
    y, x, c = here()
    to_x, to_y, to_c = {"gx": 1 - x}, {"gy": 1 - y}, {"core": 1 - c}
    chips = [(1 - y, 1 - x), (y, 1 - x), (1 - y, x), (y, x)]
    low, high = pl.ds(0, cut), pl.ds(cut, rows - cut)

    def push(k, src, dst, to):
        copy = pltpu.make_async_remote_copy(
            src_ref=src, dst_ref=dst, send_sem=send.at[k], recv_sem=recv.at[k], device_id=to, device_id_type=MESH
        )
        copy.start()
        return copy

    def add(k, extra, start, size, offset=0):
        @pl.loop(0, size // SLAB)
        def _(step):
            at = pl.ds(pl.multiple_of(start + step * SLAB, SLAB), SLAB)
            of = pl.ds(pl.multiple_of(start - offset + step * SLAB, SLAB), SLAB)
            part[k, c, at] = (part[k, c, at].astype(F32) + extra[of].astype(F32)).astype(BF16)

    loads = [pltpu.make_async_copy(left_ref.at[a * 2 + b], left.at[k], local.at[k]) for k, (a, b) in enumerate(chips)]
    load_right = pltpu.make_async_copy(right_ref, right, local.at[4])
    load_aux = [pltpu.make_async_copy(r, v, local.at[5 + k]) for k, (r, v) in enumerate(zip(aux_refs, aux))]
    loads[0].start()
    load_right.start()
    for load in loads[1:] + load_aux:
        load.start()
    if n_swap:
        greet([name for _, name in swap_peers(1, kinds)])
        swap_finish = swap_begin(1, kinds, swap_in, swap_out, *refs[13:])
    else:
        greet([to_x, to_y, to_c])

    def product(k):
        loads[k].wait()

        @pl.loop(0, width // CHIP_COLS)
        def _(step):
            at = pl.ds(pl.multiple_of(step * CHIP_COLS, CHIP_COLS), CHIP_COLS)
            here_part = dot_cols(left[k], right[at]) if across else dot(left[k], right[:, at])
            part[k, 0, :, at] = here_part[:rows].astype(BF16)
            part[k, 1, :, at] = here_part[rows:].astype(BF16)

        return push(k, part.at[k, 1 - c], got.at[k], to_c)

    load_right.wait()
    sent = [product(0), product(1)]
    sent[0].wait_recv()
    add(0, got.at[0], 0, rows)
    far_x = push(4, part.at[0, c, low], near_x, to_x)
    far_y = push(5, part.at[0, c, high], near_y, to_y)
    sent.append(product(2))
    sent[1].wait_recv()
    add(1, got.at[1], 0, rows)
    plain_x = push(6, part.at[1, c, low], from_x.at[low], to_x)
    sent[2].wait_recv()
    add(2, got.at[2], 0, rows)
    plain_y = push(7, part.at[2, c, high], from_y.at[high], to_y)
    sent.append(product(3))
    far_y.wait_recv()
    add(1, near_y, cut, rows - cut, cut)
    more_x = push(8, part.at[1, c, high], from_x.at[high], to_x)
    far_x.wait_recv()
    add(2, near_x, 0, cut)
    more_y = push(9, part.at[2, c, low], from_y.at[low], to_y)
    sent[3].wait_recv()
    for load in load_aux:
        load.wait()
    plain_x.wait_recv()
    plain_y.wait_recv()
    more_x.wait_recv()
    more_y.wait_recv()
    gains = gains_ref[...]
    acc[...] = jnp.zeros_like(acc)

    @pl.loop(0, rows // SLAB)
    def _(step):
        at = pl.ds(pl.multiple_of(step * SLAB, SLAB), SLAB)
        total = part[3, c, at].astype(F32) + got[3, at].astype(F32) + from_x[at].astype(F32) + from_y[at].astype(F32)
        held = [a[at].astype(F32) for a in aux]
        if mode == "one":
            first, normal, inverse = first_norm(by_rows(deep_alpha * held[0] + total, zs, piece), gains)
            outs[0][at] = first
            outs[1][at] = normal
            outs[2][at] = jnp.broadcast_to(inverse, (SLAB, 128))
            block[at] = first.astype(BF16)
        elif mode == "back":
            d_pre, terms, d_first = first_back(total, held[0], held[1], held[2][:, 0:1], gains)
            outs[0][at] = d_pre
            block[at] = in_order(d_pre, zs, piece).astype(BF16)
            acc[0] += terms
            acc[1] += d_first
        else:
            outs[0][at] = in_order(deep_alpha * held[0] + total, zs, piece).astype(BF16)

    if mode == "back":
        outs[-1][0:1] = jnp.sum(acc[0], axis=0, keepdims=True)
        outs[-1][1:2] = jnp.sum(acc[1], axis=0, keepdims=True)
    for copy in sent + [far_x, far_y, plain_x, plain_y, more_x, more_y]:
        copy.wait_send()
    if n_swap:
        swap_finish()
    if spread:
        spread_block(cut, 10, block, all_ref, send, recv, local.at[4])


def group_fold(name, zs, mode, left, right, gains, aux, out_types, extras=(), kinds=()):
    across = mode != "one"
    rows, depth = left.shape[0] // 8, left.shape[1]
    width = gains.shape[1]
    cut = rows // 2
    spread = mode != "last"
    out_shape = [jax.ShapeDtypeStruct((8, rows, width), BF16)] * spread + out_types
    n, n_swap = len(aux), len(extras)
    n_sems = 23 if spread else 10
    return pl.pallas_call(
        functools.partial(fold_kernel, mode, across, zs, width // (8 * zs), n, len(out_types), kinds),
        out_shape=out_shape + swap_shapes(1, extras, kinds),
        in_specs=[ANY, ANY, ROWS] + [ANY] * (n + n_swap),
        out_specs=[ANY] * spread + [ROWS] * len(out_types) + [ANY] * n_swap,
        scratch_shapes=[pltpu.VMEM(a.shape, a.dtype) for a in aux]
        + [
            pltpu.VMEM((4, 2 * rows, depth), BF16),
            pltpu.VMEM(right.shape, BF16),
            pltpu.VMEM((4, 2, rows, width), BF16),
            pltpu.VMEM((4, rows, width), BF16),
            pltpu.VMEM((cut, width), BF16),
            pltpu.VMEM((rows - cut, width), BF16),
            pltpu.VMEM((rows, width), BF16),
            pltpu.VMEM((rows, width), BF16),
            pltpu.VMEM((rows, width), BF16),
            pltpu.VMEM((2, SLAB, width), F32),
            pltpu.SemaphoreType.DMA((n_sems,)),
            pltpu.SemaphoreType.DMA((n_sems,)),
            pltpu.SemaphoreType.DMA((5 + n,)),
        ]
        + (swap_scratch(1, kinds) if n_swap else []),
        compiler_params=pltpu.CompilerParams(
            collective_id=name, has_side_effects=True, vmem_limit_bytes=50 * 2**20
        ),
        cost_estimate=pl.CostEstimate(flops=0, bytes_accessed=(200 if spread else 110) * 2**20, transcendentals=0),
    )(left.reshape(4, 2 * rows, depth), right, gains, *aux, *extras)


def turn_kernel(
    zs, piece, x_ref, in_ref, out_ref, gains_ref, first_ref, grad_ref,
    all_ref, kept_ref, right_ref, result_ref, d_pre_ref, sums_ref, dw_ref,
    first, grad, w_in, kept, left, right, part, got, near_x, near_y, from_x, from_y, whole, dw, acc,
    fold_send, fold_recv, all_send, all_recv, line_send, line_recv, local, x_local
):
    rows = first.shape[0]
    tile = left.shape[2]
    wide = right.shape[2]
    y, x, c = here()
    z = lax.axis_index("z")
    to_x, to_y, to_c = {"gx": 1 - x}, {"gy": 1 - y}, {"core": 1 - c}
    chips = [(1 - y) * 2 + 1 - x, y * 2 + 1 - x, (1 - y) * 2 + x, y * 2 + x]
    me, by_x, by_y, far = place(y, x, c), place(y, 1 - x, c), place(1 - y, x, c), place(1 - y, 1 - x, c)
    other, other_x, other_y, other_far = (
        place(y, x, 1 - c),
        place(y, 1 - x, 1 - c),
        place(1 - y, x, 1 - c),
        place(1 - y, 1 - x, 1 - c),
    )
    half = rows // 2
    most = -(-half // (2 * SLAB)) * SLAB
    lows = [(0, most), (half, half - most)]
    highs = [(most, half - most), (2 * half - most, most)]
    top, bottom = pl.ds(0, half), pl.ds(half, half)
    sent = []

    def remote(sems, k, src, dst, to):
        return pltpu.make_async_remote_copy(
            src_ref=src,
            dst_ref=dst,
            send_sem=sems[0].at[k],
            recv_sem=sems[1].at[k],
            device_id=to,
            device_id_type=MESH,
        )

    def push(sems, k, src, dst, to):
        copy = remote(sems, k, src, dst, to)
        copy.start()
        sent.append(copy)

    def landed(sems, k, dst):
        remote(sems, k, dst, dst, to_c).wait_recv()

    folds, alls, lines = (fold_send, fold_recv), (all_send, all_recv), (line_send, line_recv)

    load_out = pltpu.make_async_copy(out_ref, right.at[z], local.at[0])
    load_in = pltpu.make_async_copy(in_ref, w_in, local.at[1])
    load_first = pltpu.make_async_copy(first_ref, first, local.at[2])
    load_grad = pltpu.make_async_copy(grad_ref, grad, local.at[3])

    def load_x(g):
        return pltpu.make_async_copy(x_ref.at[g], whole.at[g], x_local.at[g])

    load_out.start()

    barrier = pltpu.get_barrier_semaphore()
    for to in (to_x, to_y, to_c):
        pl.semaphore_signal(barrier, inc=1, device_id=to, device_id_type=MESH)

    @pl.when(z > 0)
    def _():
        pl.semaphore_signal(barrier, inc=1, device_id={"z": z - 1}, device_id_type=MESH)

    @pl.when(z < zs - 1)
    def _():
        pl.semaphore_signal(barrier, inc=1, device_id={"z": z + 1}, device_id_type=MESH)

    inside = (z > 0) & (z < zs - 1)

    @pl.when(inside)
    def _():
        pl.semaphore_wait(barrier, 5)

    @pl.when(jnp.logical_not(inside))
    def _():
        pl.semaphore_wait(barrier, 4)

    def shard_of(step, up):
        return z - step if up else z + step

    def hop(step, up):
        ref = right.at[shard_of(step, up)]
        return remote(lines, 2 * step + (0 if up else 1), ref, ref, {"z": z + 1 if up else z - 1})

    def sends(step, up):
        return (z >= step) & (z < zs - 1) if up else (z <= zs - 1 - step) & (z > 0)

    def gets(step, up):
        return z >= step + 1 if up else z <= zs - 2 - step

    def line_serve(step):
        for up in (True, False):

            @pl.when(gets(step - 1, up) & sends(step, up))
            def _(up=up):
                landed(lines, 2 * (step - 1) + (0 if up else 1), right.at[shard_of(step, up)])
                hop(step, up).start()

    def line_take(step):
        for up in (True, False):

            @pl.when(gets(step - 1, up) & jnp.logical_not(sends(step, up)))
            def _(up=up):
                landed(lines, 2 * (step - 1) + (0 if up else 1), right.at[shard_of(step, up)])

    load_out.wait()
    for up in (True, False):

        @pl.when(sends(0, up))
        def _(up=up):
            hop(0, up).start()

    load_in.start()
    for g in range(8):
        load_x(g).start()


    load_in.wait()

    @pl.loop(0, 8)
    def _(g):
        @pl.when(g == 6)
        def _():
            line_serve(1)

        load_x(g).wait()
        projected = dot(whole[g], w_in[...])
        gate, up = projected[:, :tile], projected[:, tile:]
        act, slope = gate_parts(gate)
        left[g] = (act * up).astype(BF16)
        kept[g] = jnp.concatenate([up * slope, act], axis=1).astype(BF16)

    load_first.start()
    load_grad.start()
    keep = pltpu.make_async_copy(kept, kept_ref, local.at[4])
    keep.start()

    def add(k, extra, start, offset, at):
        @pl.loop(0, half // SLAB)
        def _(step):
            row = pl.ds(pl.multiple_of(start + step * SLAB, SLAB), SLAB)
            of = pl.ds(pl.multiple_of(start - offset + step * SLAB, SLAB), SLAB)
            part[k, c, row, at] = (part[k, c, row, at].astype(F32) + extra[of, at].astype(F32)).astype(BF16)

    def chip_sum(k, at):
        add(k, got.at[k], 0, 0, at)
        add(k, got.at[k], half, 0, at)

    def product(k, block, at):
        found = dot(left[pl.ds(2 * chips[k], 2)].reshape(2 * rows, tile), right[block])
        part[k, 0, :, at] = found[:rows].astype(BF16)
        part[k, 1, :, at] = found[rows:].astype(BF16)

    def block_at(i):
        if i == 0:
            return z
        below = z < zs // 2
        near = jnp.where(below, z, zs - 1 - z)
        spot = jnp.where(i <= 2 * near, jnp.where(i % 2 == 1, near - (i + 1) // 2, near + i // 2), i)
        return jnp.where(below, spot, zs - 1 - spot)

    def block_cols(i):
        return pl.ds(pl.multiple_of(block_at(i) * wide, wide), wide)

    def fold_start(i):
        b, block, at = 8 * i, block_at(i), block_cols(i)
        rest = pl.ds(1, 3)
        product(0, block, at)
        push(folds, b, part.at[0, 1 - c, :, at], got.at[0, :, at], to_c)
        for k in (1, 2, 3):
            product(k, block, at)
        push(folds, b + 1, part.at[rest, 1 - c, :, at], got.at[rest, :, at], to_c)
        landed(folds, b, got.at[0, :, at])
        chip_sum(0, at)
        push(folds, b + 2, part.at[0, c, top, at], near_x.at[:, at], to_x)
        push(folds, b + 3, part.at[0, c, bottom, at], near_y.at[:, at], to_y)
        landed(folds, b + 1, got.at[rest, :, at])
        chip_sum(1, at)
        push(folds, b + 4, part.at[1, c, top, at], from_x.at[top, at], to_x)
        chip_sum(2, at)
        push(folds, b + 5, part.at[2, c, bottom, at], from_y.at[bottom, at], to_y)

    def fold_end(i):
        b, at = 8 * i, block_cols(i)
        landed(folds, b + 3, near_y.at[:, at])
        add(1, near_y, half, half, at)
        push(folds, b + 6, part.at[1, c, bottom, at], from_x.at[bottom, at], to_x)
        landed(folds, b + 2, near_x.at[:, at])
        add(2, near_x, 0, 0, at)
        push(folds, b + 7, part.at[2, c, top, at], from_y.at[top, at], to_y)

    gains = gains_ref[...]
    line_take(1)
    fold_start(0)
    fold_start(1)
    fold_end(0)
    for i in range(2, zs):
        if i < zs - 1:
            line_serve(i)
        fold_end(i - 1)
        line_take(i)
        fold_start(i)
    fold_end(zs - 1)
    carry = pltpu.make_async_copy(right, right_ref, local.at[5])
    carry.start()
    load_first.wait()
    load_grad.wait()
    acc[...] = jnp.zeros_like(acc)
    for i in range(zs):
        at = block_cols(i)
        landed(folds, 8 * i + 4, from_x.at[top, at])
        landed(folds, 8 * i + 5, from_y.at[bottom, at])
        landed(folds, 8 * i + 6, from_x.at[bottom, at])
        landed(folds, 8 * i + 7, from_y.at[top, at])

    def low(i):
        return pl.ds(*lows[i])

    def high(i):
        return pl.ds(*highs[i])

    def span(i):
        return pl.ds(i * half, half)

    def norm(i):
        @pl.loop(0, half // SLAB)
        def _(step):
            at = pl.ds(pl.multiple_of(i * half + step * SLAB, SLAB), SLAB)
            total = part[3, c, at].astype(F32) + got[3, at].astype(F32)
            total += from_x[at].astype(F32) + from_y[at].astype(F32)
            dy = grad[at].astype(F32)
            result, d_pre, terms = second_norm(total, first[at], dy, gains)
            result_ref[at] = result.astype(BF16)
            d_pre_ref[at] = d_pre
            whole[me, at] = d_pre.astype(BF16)
            acc[0] += terms
            acc[1] += dy

        b = 13 * i
        push(alls, b, whole.at[me, low(i)], whole.at[me, low(i)], to_x)
        push(alls, b + 1, whole.at[me, high(i)], whole.at[me, high(i)], to_y)
        push(alls, b + 2, whole.at[me, high(i)], whole.at[me, high(i)], to_x)
        push(alls, b + 3, whole.at[me, low(i)], whole.at[me, low(i)], to_y)
        push(alls, b + 4, whole.at[me, span(i)], whole.at[me, span(i)], to_c)

    def pass_on(i, k, slot, at, onward):
        ref = whole.at[slot, at]
        landed(alls, 13 * i + k, ref)
        for where, to in onward:
            push(alls, 13 * i + where, ref, ref, to)

    def spread_first(i):
        pass_on(i, 0, by_x, low(i), [(5, to_y), (7, to_c)])
        pass_on(i, 1, by_y, high(i), [(6, to_x), (8, to_c)])

    def spread_rest(i):
        pass_on(i, 2, by_x, high(i), [(9, to_c)])
        pass_on(i, 3, by_y, low(i), [(10, to_c)])

    def spread_far(i):
        pass_on(i, 5, far, low(i), [(11, to_c)])
        pass_on(i, 6, far, high(i), [(12, to_c)])

    outward = []

    def gradient(k, last=False, first_one=False):
        pair = pl.ds(2 * chips[k], 2)
        outward.append(pltpu.make_async_copy(whole.at[pair], all_ref.at[pair], local.at[6 + k]))
        outward[-1].start()

        @pl.loop(0, zs)
        def _(block):
            at = pl.ds(pl.multiple_of(block * wide, wide), wide)
            found = dot_rows(left[pair].reshape(2 * rows, tile), whole[pair, :, at].reshape(2 * rows, wide))
            if first_one:
                dw[block] = found
            elif last:
                dw_ref[block] = (dw[block] + found).astype(BF16)
            else:
                dw[block] += found

    norm(0)
    norm(1)
    spread_first(0)
    for i in (0, 1):
        landed(alls, 13 * i + 4, whole.at[other, span(i)])
    gradient(3, first_one=True)
    spread_rest(0)
    spread_first(1)
    spread_rest(1)
    for i in (0, 1):
        landed(alls, 13 * i + 7, whole.at[other_x, low(i)])
        landed(alls, 13 * i + 9, whole.at[other_x, high(i)])
    gradient(1)
    spread_far(0)
    for i in (0, 1):
        landed(alls, 13 * i + 8, whole.at[other_y, high(i)])
        landed(alls, 13 * i + 10, whole.at[other_y, low(i)])
    gradient(2)
    sums_ref[0:1] = jnp.sum(acc[0], axis=0, keepdims=True)
    sums_ref[1:2] = jnp.sum(acc[1], axis=0, keepdims=True)
    spread_far(1)
    for i in (0, 1):
        landed(alls, 13 * i + 11, whole.at[other_far, low(i)])
        landed(alls, 13 * i + 12, whole.at[other_far, high(i)])
    gradient(0, last=True)
    for copy in outward + [keep, carry]:
        copy.wait()
    for copy in sent:
        copy.wait_send()
    for step in range(zs - 1):
        for up in (True, False):

            @pl.when(sends(step, up))
            def _(step=step, up=up):
                hop(step, up).wait_send()


def turn(zs, x, w_in, w_out, gains, first, grad):
    rows = x.shape[0] // 8
    units, wide = w_out.shape
    width = gains.shape[1]
    half = rows // 2
    by_z = (zs, units, wide)
    return pl.pallas_call(
        functools.partial(turn_kernel, zs, width // (8 * zs)),
        out_shape=[
            jax.ShapeDtypeStruct((8, rows, width), BF16),
            jax.ShapeDtypeStruct((8, rows, 2 * units), BF16),
            jax.ShapeDtypeStruct(by_z, BF16),
            jax.ShapeDtypeStruct((rows, width), BF16),
            jax.ShapeDtypeStruct((rows, width), F32),
            jax.ShapeDtypeStruct((8, width), F32),
            jax.ShapeDtypeStruct(by_z, BF16),
        ],
        in_specs=[ANY, ANY, ANY, ROWS, ANY, ANY],
        out_specs=[ANY] * 3 + [ROWS] * 4,
        scratch_shapes=[
            pltpu.VMEM((rows, width), F32),
            pltpu.VMEM((rows, width), BF16),
            pltpu.VMEM(w_in.shape, BF16),
            pltpu.VMEM((8, rows, 2 * units), BF16),
            pltpu.VMEM((8, rows, units), BF16),
            pltpu.VMEM(by_z, BF16),
            pltpu.VMEM((4, 2, rows, width), BF16),
            pltpu.VMEM((4, rows, width), BF16),
            pltpu.VMEM((half, width), BF16),
            pltpu.VMEM((half, width), BF16),
            pltpu.VMEM((rows, width), BF16),
            pltpu.VMEM((rows, width), BF16),
            pltpu.VMEM((8, rows, width), BF16),
            pltpu.VMEM(by_z, F32),
            pltpu.VMEM((2, SLAB, width), F32),
            pltpu.SemaphoreType.DMA((8 * zs,)),
            pltpu.SemaphoreType.DMA((8 * zs,)),
            pltpu.SemaphoreType.DMA((26,)),
            pltpu.SemaphoreType.DMA((26,)),
            pltpu.SemaphoreType.DMA((2 * (zs - 1),)),
            pltpu.SemaphoreType.DMA((2 * (zs - 1),)),
            pltpu.SemaphoreType.DMA((10,)),
            pltpu.SemaphoreType.DMA((8,)),
        ],
        compiler_params=pltpu.CompilerParams(collective_id=1, has_side_effects=True, vmem_limit_bytes=60 * 2**20),
        cost_estimate=pl.CostEstimate(flops=0, bytes_accessed=380 * 2**20, transcendentals=0),
    )(x.reshape(8, rows, width), w_in, w_out, gains, first, grad)


def swap_kernel(zs, kinds, *refs):
    n = len(kinds)
    greet([name for _, name in swap_peers(zs, kinds)])
    swap_begin(zs, kinds, refs[:n], refs[n : 2 * n], *refs[2 * n :])()


def group_swap(name, zs, arrays, kinds):
    n = len(arrays)
    return pl.pallas_call(
        functools.partial(swap_kernel, zs, kinds),
        out_shape=swap_shapes(zs, arrays, kinds),
        in_specs=[ANY] * n,
        out_specs=[ANY] * n,
        scratch_shapes=swap_scratch(zs, kinds),
        compiler_params=pltpu.CompilerParams(collective_id=name, has_side_effects=True),
        cost_estimate=pl.CostEstimate(flops=0, bytes_accessed=50 * 2**20, transcendentals=0),
    )(*arrays)


def enter_kernel(zs, kinds, x_ref, grad_ref, *refs):
    n = len(kinds)
    blocks, x_all, grad_out, outs, refs = refs[:n], refs[n], refs[n + 1], refs[n + 2 : 2 * n + 2], refs[2 * n + 2 :]
    x_rows, sems = refs[0], refs[1:]
    rows, width = x_ref.shape
    greet([name for _, name in swap_peers(zs, kinds)])
    finish = swap_begin(zs, kinds, blocks, outs, *sems[:3])
    for ref, out in ((x_ref, x_rows), (grad_ref, grad_out)):

        @pl.loop(0, rows // SLAB)
        def _(step, ref=ref, out=out):
            at = pl.ds(pl.multiple_of(step * SLAB, SLAB), SLAB)
            out[at] = by_rows(ref[at].astype(F32), zs, width // (8 * zs)).astype(BF16)

    spread_block(rows // 2, 0, x_rows, x_all, *sems[3:])
    finish()


def enter(zs, x, grad, arrays, kinds):
    n = len(arrays)
    return pl.pallas_call(
        functools.partial(enter_kernel, zs, kinds),
        out_shape=[jax.ShapeDtypeStruct((8,) + x.shape, x.dtype), jax.ShapeDtypeStruct(grad.shape, grad.dtype)]
        + swap_shapes(zs, arrays, kinds),
        in_specs=[ROWS] * 2 + [ANY] * n,
        out_specs=[ANY, ROWS] + [ANY] * n,
        scratch_shapes=[pltpu.VMEM(x.shape, x.dtype)]
        + swap_scratch(zs, kinds)
        + [pltpu.SemaphoreType.DMA((13,)), pltpu.SemaphoreType.DMA((13,)), pltpu.SemaphoreType.DMA],
        compiler_params=pltpu.CompilerParams(collective_id=3, has_side_effects=True, vmem_limit_bytes=56 * 2**20),
        cost_estimate=pl.CostEstimate(flops=0, bytes_accessed=150 * 2**20, transcendentals=0),
    )(x, grad, *arrays)


def ff_kernel(x_ref, w_ref, hidden_ref, kept_ref):
    tile = hidden_ref.shape[1]
    projected = dot(x_ref[...], w_ref[...])
    gate, up = projected[:, :tile], projected[:, tile:]
    act, slope = gate_parts(gate)
    hidden_ref[...] = (act * up).astype(BF16)
    kept_ref[...] = jnp.concatenate([up * slope, act], axis=1).astype(BF16)


def ff_back_kernel(grad_ref, w_ref, kept_ref, out_ref):
    zs, _, wide = w_ref.shape
    d_hidden = dot_cols(grad_ref[:, :wide], w_ref[0])
    for z in range(1, zs):
        d_hidden += dot_cols(grad_ref[:, z * wide : (z + 1) * wide], w_ref[z])
    out_ref[...] = (jnp.concatenate([d_hidden, d_hidden], axis=1) * kept_ref[...].astype(F32)).astype(BF16)


FF_ROWS = 256


def ff_rows(width):
    return pl.BlockSpec((FF_ROWS, width), lambda i: (i, 0))


def ff_forward(x, w):
    rows, depth = x.shape
    wide = w.shape[1]
    return pl.pallas_call(
        ff_kernel,
        grid=(rows // FF_ROWS,),
        in_specs=[ff_rows(depth), pl.BlockSpec((depth, wide), lambda i: (0, 0))],
        out_specs=[ff_rows(wide // 2), ff_rows(wide)],
        out_shape=[jax.ShapeDtypeStruct((rows, wide // 2), BF16), jax.ShapeDtypeStruct((rows, wide), BF16)],
        compiler_params=PARAMS,
        cost_estimate=pl.CostEstimate(flops=2 * rows * depth * wide, bytes_accessed=20 * 2**20, transcendentals=0),
    )(x, w)


def ff_backward(grad, w, kept):
    rows, depth = grad.shape
    wide = kept.shape[1]
    return pl.pallas_call(
        ff_back_kernel,
        grid=(rows // FF_ROWS,),
        in_specs=[ff_rows(depth), pl.BlockSpec(w.shape, lambda i: (0, 0, 0)), ff_rows(wide)],
        out_specs=ff_rows(wide),
        out_shape=jax.ShapeDtypeStruct((rows, wide), BF16),
        compiler_params=PARAMS,
        cost_estimate=pl.CostEstimate(flops=rows * depth * wide, bytes_accessed=20 * 2**20, transcendentals=0),
    )(grad, w, kept)


def cut_kernel(in_ref, out_ref, in_blocks, out_blocks, wide):
    group, _, double = in_blocks.shape
    tile, ff = double // 2, out_ref.shape[1]
    span = group * tile
    odd = ff % 128
    live = lax.broadcasted_iota(jnp.int32, (in_ref.shape[0], span), 1) < ff
    wide[...] = jnp.zeros_like(wide)
    wide[:, : 2 * ff] = in_ref[...].astype(F32)
    gate = jnp.where(live, wide[:, :span], 0.0)
    up = pltpu.roll(wide[:, ff - odd : ff - odd + span], span - odd, 1)
    up = jnp.where(live, up, 0.0)
    wide[:, :span] = jnp.zeros_like(live, F32)
    wide[:, :ff] = out_ref[...].astype(F32)
    down = wide[:, :span]
    for g in range(group):
        at = slice(g * tile, (g + 1) * tile)
        in_blocks[g] = jnp.concatenate([gate[:, at], up[:, at]], axis=1).astype(BF16)
        out_blocks[g] = down[:, at].astype(BF16)


def cut_ff(w_in, w_out, group, tile):
    rows, ff = w_out.shape
    return pl.pallas_call(
        cut_kernel,
        grid=(rows // 16,),
        in_specs=[pl.BlockSpec((16, 2 * ff), lambda i: (i, 0)), pl.BlockSpec((16, ff), lambda i: (i, 0))],
        out_specs=[
            pl.BlockSpec((group, 16, 2 * tile), lambda i: (0, i, 0)),
            pl.BlockSpec((group, 16, tile), lambda i: (0, i, 0)),
        ],
        out_shape=[
            jax.ShapeDtypeStruct((group, rows, 2 * tile), BF16),
            jax.ShapeDtypeStruct((group, rows, tile), BF16),
        ],
        scratch_shapes=[pltpu.VMEM((16, -(-(ff + group * tile) // 128) * 128), F32)],
        compiler_params=PARAMS,
    )(w_in, w_out)


def join_kernel(in_blocks, out_blocks, in_ref, out_ref):
    group, _, double = in_blocks.shape
    tile, ff = double // 2, out_ref.shape[1]
    odd = ff % 128
    blocks = [in_blocks[g].astype(F32) for g in range(group)]
    gate = jnp.concatenate([block[:, :tile] for block in blocks], axis=1)
    up = jnp.concatenate([block[:, tile:] for block in blocks], axis=1)
    up = pltpu.roll(up, odd, 1)
    lane = lax.broadcasted_iota(jnp.int32, (up.shape[0], 128), 1)
    in_ref[:, : ff - odd] = gate[:, : ff - odd]
    in_ref[:, ff - odd : ff - odd + 128] = jnp.where(lane < odd, gate[:, ff - odd : ff - odd + 128], up[:, :128])
    in_ref[:, ff - odd + 128 :] = up[:, 128 : ff + odd]
    down = jnp.concatenate([out_blocks[g].astype(F32) for g in range(group)], axis=1)
    out_ref[...] = down[:, :ff]


def join_ff(in_blocks, out_blocks, ff):
    group, rows, tile = out_blocks.shape
    return pl.pallas_call(
        join_kernel,
        grid=(rows // 16,),
        in_specs=[
            pl.BlockSpec((group, 16, 2 * tile), lambda i: (0, i, 0)),
            pl.BlockSpec((group, 16, tile), lambda i: (0, i, 0)),
        ],
        out_specs=[pl.BlockSpec((16, 2 * ff), lambda i: (i, 0)), pl.BlockSpec((16, ff), lambda i: (i, 0))],
        out_shape=[jax.ShapeDtypeStruct((rows, 2 * ff), F32), jax.ShapeDtypeStruct((rows, ff), F32)],
        compiler_params=PARAMS,
    )(in_blocks, out_blocks)


def closing_kernel(zs, sum_ref, rows_ref, qkv_ref, dense_ref, total_ref, got, mine, lines, *refs):
    send, recv, local, line_send, line_recv = refs
    y, x, c = here()
    z = lax.axis_index("z")
    me = place(y, x, c)
    wide = got.shape[2]
    width = wide // 3
    piece = got.shape[1]
    found = swap_peers(zs, ("line",))
    greet([name for _, name in found])
    copies, comes = [], []
    for k, (peer, name) in enumerate(found[:7]):
        sems = dict(send_sem=send.at[k], recv_sem=recv.at[k], device_id=name, device_id_type=MESH)
        src = rows_ref.at[peer, :, pl.ds(0, wide)]
        copies.append(pltpu.make_async_remote_copy(src_ref=src, dst_ref=got.at[me], **sems))
        comes.append(pltpu.make_async_remote_copy(src_ref=got.at[peer], dst_ref=got.at[peer], **sems))
    for k, (peer, name) in enumerate(found[7:]):
        sems = dict(send_sem=line_send.at[k], recv_sem=line_recv.at[k], device_id=name, device_id_type=MESH)
        copies.append(pltpu.make_async_remote_copy(src_ref=sum_ref, dst_ref=lines.at[z], **sems))
        comes.append(pltpu.make_async_remote_copy(src_ref=lines.at[peer], dst_ref=lines.at[peer], **sems))
    for copy in copies:
        copy.start()
    keeps = [
        pltpu.make_async_copy(rows_ref.at[me, :, pl.ds(0, wide)], got.at[me], local.at[0]),
        pltpu.make_async_copy(sum_ref, lines.at[z], local.at[1]),
        pltpu.make_async_copy(rows_ref.at[:, :, pl.ds(wide, width)], mine, local.at[2]),
    ]
    for keep in keeps:
        keep.start()
    keeps[2].wait()
    for at in range(0, piece, 16):
        rows = jnp.concatenate([mine[g, at : at + 16] for g in range(8)], axis=1).astype(F32)
        dense_ref[at : at + 16] = rows
    for come in comes:
        come.wait_recv()
    for keep in keeps[:2]:
        keep.wait()
    for g in range(8):
        for j in range(3):
            at = pl.ds(j * D + g * width, width)
            qkv_ref[:, at] = got[g, :, j * width : (j + 1) * width].astype(F32)
    total = lines[0]
    for k in range(1, zs):
        total += lines[k]
    part = total[:, :piece]
    for k in range(1, zs):
        part = jnp.where(z == k, total[:, k * piece : (k + 1) * piece], part)
    total_ref[...] = part
    for copy in copies:
        copy.wait_send()


def closing(zs, sums, rows):
    _, piece, columns = rows.shape
    width = columns // 4
    return pl.pallas_call(
        functools.partial(closing_kernel, zs),
        out_shape=[
            jax.ShapeDtypeStruct((piece, 3 * D), F32),
            jax.ShapeDtypeStruct((piece, D), F32),
            jax.ShapeDtypeStruct((8, piece), F32),
        ],
        in_specs=[ROWS, ANY],
        out_specs=[ROWS] * 3,
        scratch_shapes=[
            pltpu.VMEM((8, piece, 3 * width), BF16),
            pltpu.VMEM((8, piece, width), BF16),
            pltpu.VMEM((zs, 8, width), F32),
            pltpu.SemaphoreType.DMA((7,)),
            pltpu.SemaphoreType.DMA((7,)),
            pltpu.SemaphoreType.DMA((3,)),
            pltpu.SemaphoreType.DMA((zs - 1,)),
            pltpu.SemaphoreType.DMA((zs - 1,)),
        ],
        compiler_params=pltpu.CompilerParams(collective_id=5, has_side_effects=True, vmem_limit_bytes=56 * 2**20),
        cost_estimate=pl.CostEstimate(flops=0, bytes_accessed=50 * 2**20, transcendentals=0),
    )(sums, rows)


def on_device(sizes, x_in, d_out, w_qkv, w_dense, w_in, w_out, gone, bone, gtwo, btwo, flags, span_start, span_len):
    gy, gx, cores, zs = sizes
    piece = w_qkv.shape[0]
    ff = w_out.shape[1]
    group = gy * gx * cores
    width = D // group
    tile = -(-ff // (group * 64)) * 64
    own = gy == 2

    def permute(array):
        lead = array.shape[:-1]
        return jnp.swapaxes(array.reshape(lead + (group, zs, piece)), -3, -2).reshape(lead + (D,))

    def restore(array):
        lead = array.shape[:-1]
        return jnp.swapaxes(array.reshape(lead + (zs, group, piece)), -3, -2).reshape(lead + (D,))

    def swap(name, arrays, kinds):
        if own:
            return group_swap(name, zs, arrays, kinds)
        ways = {
            "swap": lambda a: lax.all_to_all(a, GROUP, 0, 0, tiled=True),
            "group": lambda a: lax.all_gather(a, GROUP, axis=0),
            "line": lambda a: lax.all_gather(a, "z", axis=0),
        }
        return [ways[k](a) for a, k in zip(arrays, kinds)]

    def spread_rows(block):
        return lax.all_gather(block, GROUP, axis=0, tiled=True)

    rows_f32 = jax.ShapeDtypeStruct((SEQ_LEN, D), F32)
    rows_low = jax.ShapeDtypeStruct((SEQ_LEN, D), BF16)
    sums_type = jax.ShapeDtypeStruct((8, D), F32)

    def fold(partial):
        return lax.psum_scatter(partial.astype(BF16), GROUP, scatter_dimension=0, tiled=True).astype(F32)

    def stack_sums(*arrays):
        return jnp.pad(jnp.stack([jnp.sum(a, axis=0) for a in arrays]), ((0, 6), (0, 0)))

    def fold_one(left, right, x, gains):
        if own:
            kinds = [rows_f32, rows_f32, jax.ShapeDtypeStruct((SEQ_LEN, 128), F32)]
            whole, first, normal, inverse = group_fold(0, zs, "one", left, right, gains, [x], kinds)
            return whole.reshape(left.shape[0], D), first, normal, inverse
        first, normal, inverse = first_norm(permute(deep_alpha * x.astype(F32) + fold(dot(left, right))), gains)
        return spread_rows(first.astype(BF16)), first, normal, inverse

    def ff_turn(x, w_in, w_out, first, grad, gains):
        if own:
            whole, kept, w_out, result, d_pre, sums, d_out = turn(zs, x, w_in, w_out, gains, first, grad)
            rows = x.shape[0]
            return whole.reshape(rows, D), kept.reshape(rows, -1), w_out, result, d_pre, sums, d_out
        w_out = lax.all_gather(w_out, "z", axis=0)
        hidden, kept = ff_forward(x, w_in)
        grad = grad.astype(F32)
        right = jnp.swapaxes(w_out, 0, 1).reshape(-1, D)
        result, d_pre, terms = second_norm(fold(dot(hidden, right)), first, grad, gains)
        whole = spread_rows(d_pre.astype(BF16))
        d_out = jnp.swapaxes(dot_rows(hidden, whole).reshape(-1, zs, D // zs), 0, 1).astype(BF16)
        return whole, kept, w_out, result.astype(BF16), d_pre, stack_sums(terms, grad), d_out

    def fold_back(left, right, d_pre_two, normal, inverse, gains):
        if own:
            kinds = [rows_f32, sums_type]
            whole, d_pre, sums = group_fold(7, zs, "back", left, right, gains, [d_pre_two, normal, inverse], kinds)
            return whole.reshape(left.shape[0], D), d_pre, sums
        d_pre, terms, d_first = first_back(fold(dot_cols(left, right)), d_pre_two, normal, inverse, gains)
        return spread_rows(restore(d_pre).astype(BF16)), d_pre, stack_sums(terms, d_first)

    def fold_last(left, right, d_pre, gains, extras, kinds):
        if own:
            return group_fold(8, zs, "last", left, right, gains, [d_pre], [rows_low], extras, kinds)
        out = restore((deep_alpha * d_pre + fold(dot_cols(left, right))).astype(BF16))
        return [out] + swap(8, extras, kinds)

    def gather(block):
        return lax.all_gather(block, "z", axis=0, tiled=True)

    def scatter(partial):
        return lax.psum_scatter(partial.astype(BF16), "z", scatter_dimension=0, tiled=True)

    masked = jnp.max(flags) > 0
    prefix = jnp.where(masked, SEQ_LEN, SEQ_LEN - span_len[0])
    info = jnp.concatenate([gone, bone, gtwo, btwo, jnp.stack([prefix, span_start[0]]).astype(BF16)])
    info = jnp.pad(info[None, :], ((0, 15), (0, -info.shape[0] % 128)))

    qkv_blocks = jnp.moveaxis(w_qkv.reshape(piece, 3, group, width), 2, 0).reshape(group, piece, 3 * width)
    w_dense_part = gather(w_dense)
    qkv_blocks, info = swap(2, [qkv_blocks, info], ("swap", "group"))
    w_qkv_part = gather(qkv_blocks.reshape(group * piece, 3 * width))
    info = info[:, 0]
    place_info = info[:, 4 * piece : 4 * piece + 2].astype(jnp.int32)
    prefix, start = place_info[:, 0], place_info[:, 1]
    cosine, sine = tables(prefix, start)
    in_blocks, out_blocks = cut_ff(w_in, w_out, group, tile)
    info = jnp.pad(info, ((0, -group % 16), (0, 0)))
    in_blocks, out_blocks, qkv_blocks, w_dense_part, cosine, sine = lax.optimization_barrier(
        (in_blocks, out_blocks, qkv_blocks, w_dense_part, cosine, sine)
    )
    swapped, kinds = [in_blocks, out_blocks, info], ("swap", "swap", "line")
    if own:
        x_all, grad_two, in_blocks, out_blocks, info = enter(zs, x_in, d_out, swapped, kinds)
        x_all = x_all.reshape(group * SEQ_LEN, D)
    else:
        x_all, grad_two = spread_rows(permute(x_in)), permute(d_out)
        in_blocks, out_blocks, info = swap(3, swapped, kinds)
    w_in_part = gather(in_blocks.reshape(group * piece, 2 * tile))
    out_rows = out_blocks.reshape(group * piece, tile).T
    gains = info[:, :group, : 4 * piece].astype(F32).reshape(zs, group, 4, piece)
    gains = jnp.pad(jnp.transpose(gains, (2, 0, 1, 3)).reshape(4, D), ((0, 4), (0, 0)))
    w_qkv_part, x_all, gains, out_rows = lax.optimization_barrier((w_qkv_part, x_all, gains, out_rows))
    packed = dot(x_all, w_qkv_part)
    qkv, context = attend(prefix, packed, cosine, sine)
    first_all, first, normal_one, inverse_one = fold_one(context, w_dense_part, x_in, gains)
    d_branch, kept, w_out_part, layer_out, d_pre_two, sums_two, d_w_out = ff_turn(
        first_all, w_in_part, out_rows, first, grad_two, gains
    )
    layer_out = restore(layer_out)
    d_w_out = lax.psum_scatter(d_w_out, "z", scatter_dimension=0)
    d_projected = ff_backward(d_branch, w_out_part, kept)
    d_w_in = dot_rows(first_all, d_projected).astype(BF16)
    d_w_in, d_projected = lax.optimization_barrier((d_w_in, d_projected))
    d_w_in = scatter(d_w_in)
    d_attn, d_pre_one, sums_one = fold_back(d_projected, w_in_part, d_pre_two, normal_one, inverse_one, gains)
    d_attn, d_w_out = lax.optimization_barrier((d_attn, d_w_out))
    d_context = dot_cols(d_attn, w_dense_part).astype(BF16)
    d_packed = attend_back(prefix, qkv, d_context, cosine, sine)
    d_w_qkv = dot_rows(x_all, d_packed).astype(BF16)
    d_dense = dot_rows(context, d_attn).astype(BF16).reshape(zs, piece, group, width)
    d_dense = jnp.swapaxes(d_dense, 1, 2).reshape(D, width)
    d_w_qkv = jnp.concatenate([d_w_qkv, d_dense], axis=1)
    sums = jnp.concatenate([sums_one[:2], sums_two[:2], jnp.zeros((4, D), F32)])
    d_packed, d_w_qkv, d_w_in, sums = lax.optimization_barrier((d_packed, d_w_qkv, d_w_in, sums))
    d_w_qkv = scatter(d_w_qkv)
    d_w_in, d_w_out = d_w_in.reshape(group, piece, 2 * tile), d_w_out.T.reshape(group, piece, tile)
    d_input, d_w_in, d_w_out, sums = fold_last(
        d_packed, w_qkv_part, d_pre_one, gains, [d_w_in, d_w_out, sums], ("swap", "swap", "group")
    )
    sums = jnp.sum(sums, axis=0).reshape(8, zs, group, piece)
    sums = lax.dynamic_index_in_dim(sums, lax.axis_index(GROUP), 2, keepdims=False).reshape(8, width)
    out_in, out_out = join_ff(d_w_in, d_w_out, ff)
    out_in, out_out, d_input, d_w_qkv, sums = lax.optimization_barrier((out_in, out_out, d_input, d_w_qkv, sums))
    if own:
        out_qkv, out_dense, sums = closing(zs, sums, d_w_qkv.reshape(group, piece, 4 * width))
    else:
        out_dense = d_w_qkv[:, 3 * width :].reshape(group, piece, width)
        out_dense = jnp.swapaxes(out_dense, 0, 1).reshape(piece, D).astype(F32)
        d_w_qkv = d_w_qkv[:, : 3 * width].reshape(group, piece, 3 * width)
        d_w_qkv, sums = swap(5, [d_w_qkv, sums], ("swap", "line"))
        out_qkv = jnp.transpose(d_w_qkv.astype(F32).reshape(group, piece, 3, width), (1, 2, 0, 3))
        out_qkv = out_qkv.reshape(piece, 3 * D)
        sums = jnp.sum(sums, axis=0).reshape(8, zs, piece)
        sums = lax.dynamic_index_in_dim(sums, lax.axis_index("z"), 1, keepdims=False)
    return layer_out, d_input, out_qkv, out_dense, out_in, out_out, sums[0], sums[1], sums[2], sums[3]


def solution(mesh):
    grp, shard = mesh.shape["grp"], mesh.shape["shard"]
    sizes = (grp // 4, 2, 2, shard)
    inner = Mesh(mesh.devices.reshape(sizes), ALL)
    rows, flat = P(ALL, None), P(ALL)
    return jax.shard_map(
        functools.partial(on_device, sizes),
        mesh=inner,
        in_specs=(rows,) * 6 + (flat,) * 7,
        out_specs=(rows,) * 6 + (flat,) * 4,
        check_vma=False,
    )
```

profile of v0, /device:TPU:0, one launch (start us, length us, event | category | flops | bytes accessed | tf_op | source)
XLA Modules:
  0.0 587.6 jit_solution(16683147629598688595)
XLA Ops:
  14.8 15.4 %shard_map.204 = (bf16[8,64,768]{2,1,0:T(8,128)(2,1)}, bf16[8,16,384]{2,1,0:T(8,128)(2,1)}) custom-call(bf16[8,64,768]{2,1,0:T(8,128)(2,1)} %reshape.214.refs_0_, bf16[16,384]{1,0:T(8,128)(2,1)} %pad.15.refs_1_), custom_call_target="tpu_custom_call" | custom-call | bytes 52428800 | tf_op jit(solution)/shard_map/pallas_call | solution.py:872
  31.8 4.1 shard_map.205
  36.2 5.0 sine_multiply_fusion
  41.2 65.1 %shard_map.206 = (bf16[8,224,2048]{2,1,0:T(8,128)(2,1)}, bf16[224,2048]{1,0:T(8,128)(2,1)}, bf16[8,64,1408]{2,1,0:T(8,128)(2,1)}, bf16[8,64,704]{2,1,0:T(8,128)(2,1)}, bf16[4,16,384]{2,1,0:T(8,128)(2,1)}) custom-call(bf16[224,2048]{1,0:T(8,128)(2,1)} %refs_3_.1, bf16[224,2048]{1,0:T(8,128)(2,1)} %grad_ref.1, bf16[8,64,1408]{2,1,0:T(8,128)(2,1)} %get-tuple-element.70.refs_0_, ...), custom_call_target="tpu_custom_call" | custom-call | bytes 157286400 | tf_op jit(solution)/shard_map/pallas_call | solution.py:903
  107.4 2.3 copy.34
  109.7 11.0 %fusion.4.packed_ref = f32[1792,768]{1,0:T(8,128)} fusion(bf16[1792,2048]{1,0:T(8,128)(2,1)} %bitcast.85, bf16[2048,768]{1,0:T(8,128)(2,1)} %all-gather.4.cloned.1.call-done.refs_1_), kind=kOutput, calls=%fused_computation.31 | convolution fusion | flops 5637144576 | bytes 15990784 | tf_op jit(solution)/shard_map/dot_general | solution.py:28
  120.7 11.0 %shard_map.207 = (bf16[1792,768]{1,0:T(8,128)(2,1)}, bf16[1792,256]{1,0:T(8,128)(2,1)}) custom-call(s32[8]{0:T(128)} %copy-done.13, f32[1792,768]{1,0:T(8,128)} %fusion.4.packed_ref, f32[8,224,128]{2,1,0:T(8,128)} %get-tuple-element.77.cos_ref, f32[8,224,128]{2,1,0:T(8,128)} %get-tuple-element.78.sin_ref), custom_call_target="tpu_custom_call" | custom-call | tf_op jit(solution)/shard_map/pallas_call | solution.py:112
  132.9 79.3 %shard_map.208 = (bf16[8,224,2048]{2,1,0:T(8,128)(2,1)}, f32[224,2048]{1,0:T(8,128)}, f32[224,2048]{1,0:T(8,128)}, f32[224,128]{1,0:T(8,128)S(1)}) custom-call(bf16[4,448,256]{2,1,0:T(8,128)(2,1)S(1)} %bitcast.60, bf16[256,2048]{1,0:T(8,128)(2,1)S(1)} %copy-done.7, f32[8,2048]{1,0:T(8,128)S(1)} %pad_convert_fusion.refs_2_.gains_ref, ...), custom_call_target="tpu_custom_call" | custom-call | bytes 209715200 | tf_op jit(solution)/shard_map/pallas_call | solution.py:466
  212.2 104.6 %shard_map.209 = (bf16[8,224,2048]{2,1,0:T(8,128)(2,1)}, bf16[8,224,1408]{2,1,0:T(8,128)(2,1)}, bf16[4,704,512]{2,1,0:T(8,128)(2,1)}, bf16[224,2048]{1,0:T(8,128...) custom-call(bf16[8,224,2048]{2,1,0:T(8,128)(2,1)} %get-tuple-element.82.x_ref, ...), custom_call_target="tpu_custom_call" | custom-call | bytes 398458880 | tf_op jit(solution)/shard_map/pallas_call | solution.py:821
  317.0 13.1 %shard_map.210 = bf16[1792,1408]{1,0:T(8,128)(2,1)} custom-call(bf16[1792,2048]{1,0:T(8,128)(2,1)} %bitcast.67, bf16[4,704,512]{2,1,0:T(8,128)(2,1)} %get-tuple-element.90.w_ref, bf16[1792,1408]{1,0:T(8,128)(2,1)} %bitcast.68), custom_call_target="tpu_custom_call" | custom-call | flops 5167382528 | bytes 20971520 | tf_op jit(solution)/shard_map/pallas_call | solution.py:958
  330.1 17.0 %convolution_convert_fusion = bf16[2048,1408]{1,0:T(8,128)(2,1)} fusion(bf16[1792,2048]{1,0:T(8,128)(2,1)} %bitcast.66, bf16[1792,1408]{1,0:T(8,128)(2,1)} %shard_map.210), kind=kOutput, calls=%fused_computation | convolution fusion | flops 10337648640 | bytes 18153472 | tf_op jit(solution)/shard_map/dot_general | solution.py:32
  348.6 82.8 %shard_map.211 = (bf16[8,224,2048]{2,1,0:T(8,128)(2,1)}, f32[224,2048]{1,0:T(8,128)S(1)}, f32[8,2048]{1,0:T(8,128)S(1)}) custom-call(bf16[4,448,1408]{2,1,0:T(8,128)(2,1)} %bitcast.64, bf16[2048,1408]{1,0:T(8,128)(2,1)} %all-gather.8.cloned.1.call-done.in_ref.refs_1_, f32[8,2048]{1,0:T(8,128)S(1)} %copy-done.6, f32[224,2048]{1,0:T(8,128)S(1)} %copy-done.4, ...), custom_call_target="tpu_custom_call" | custom-call | bytes 209715200 | tf_op jit(solution)/shard_map/pallas_call | solution.py:466
  432.7 5.2 convolution_convert_fusion.2
  439.1 6.1 %convolution_convert_fusion.3.d_context_ref = bf16[1792,256]{1,0:T(8,128)(2,1)} fusion(bf16[1792,2048]{1,0:T(8,128)(2,1)} %bitcast.63, bf16[256,2048]{1,0:T(8,128)(2,1)S(1)} %copy-done.8), kind=kOutput, calls=%fused_computation.4 | convolution fusion | flops 1879506944 | bytes 9306112 | tf_op jit(solution)/shard_map/dot_general | solution.py:36
  445.2 15.0 %shard_map.212 = bf16[1792,768]{1,0:T(8,128)(2,1)} custom-call(s32[8]{0:T(128)} %copy-done.13, bf16[1792,768]{1,0:T(8,128)(2,1)} %get-tuple-element.88.qkv_ref, bf16[1792,256]{1,0:T(8,128)(2,1)} %convolution_convert_fusion.3.d_context_ref, f32[8,224,128]{2,1,0:T(8,128)} %get-tuple-element.77.cos_ref, f32[8,224,128]{2,1,0:T(8,128)} %get-tuple-element.78.sin_ref), custom_call_target="tpu_custom_call" | custom-call | tf_op jit(solution)/shard_map/pallas_call | solution.py:127
  460.3 9.2 %convolution_convert_fusion.1 = bf16[2048,768]{0,1:T(8,128)(2,1)S(1)} fusion(bf16[1792,2048]{1,0:T(8,128)(2,1)} %bitcast.86, bf16[1792,768]{1,0:T(8,128)(2,1)} %shard_map.212), kind=kOutput, calls=%fused_computation.2 | convolution fusion | flops 5638717440 | bytes 13238272 | tf_op jit(solution)/shard_map/dot_general | solution.py:32
  469.5 2.3 pad_maximum_fusion
  471.7 5.4 reduce-scatter.6.cloned.1.call-done
  479.3 65.7 %shard_map.213 = (bf16[224,2048]{1,0:T(8,128)(2,1)S(1)}, bf16[8,64,1408]{2,1,0:T(8,128)(2,1)}, bf16[8,64,704]{2,1,0:T(8,128)(2,1)S(1)}, f32[8,8,2048]{2,1,0:T(8,128)S(1)}) custom-call(bf16[4,448,768]{2,1,0:T(8,128)(2,1)} %bitcast.65, bf16[2048,768]{1,0:T(8,128)(2,1)} %all-gather.4.cloned.1.call-done.refs_1_, f32[8,2048]{1,0:T(8,128)S(1)} %copy-done.6, ...), custom_call_target="tpu_custom_call" | custom-call | bytes 115343360 | tf_op jit(solution)/shard_map/pallas_call | solution.py:466
  546.8 4.5 shard_map.214
  551.2 5.3 reduce-scatter.8.cloned.1.call-done
  556.5 2.3 copy.40
  558.8 15.9 %shard_map.215 = (f32[64,6144]{1,0:T(8,128)}, f32[64,2048]{1,0:T(8,128)}, f32[8,64]{1,0:T(8,128)}) custom-call(f32[8,256]{1,0:T(8,128)} %reshape.235.sum_ref, bf16[8,64,1024]{2,1,0:T(8,128)(2,1)} %bitcast.70), custom_call_target="tpu_custom_call" | custom-call | bytes 52428800 | tf_op jit(solution)/shard_map/pallas_call | solution.py:1094
  577.0 2.7 copy.54
  (93 shorter events, 20.8 us)
Async XLA Ops:
  7.2 4.9 copy-start.14
  7.2 6.8 %copy-start.15 = (bf16[64]{0:T(256)(128)(2,1)S(1)}, bf16[64]{0:T(256)(128)(2,1)}, u32[]{:S(2)}) copy-start(bf16[64]{0:T(256)(128)(2,1)} %param.19) | copy-start | bytes 388
  7.2 6.8 %copy-start.16 = (bf16[64]{0:T(256)(128)(2,1)S(1)}, bf16[64]{0:T(256)(128)(2,1)}, u32[]{:S(2)}) copy-start(bf16[64]{0:T(256)(128)(2,1)} %param.20) | copy-start | bytes 388
  7.2 6.8 %copy-start.17 = (bf16[64]{0:T(256)(128)(2,1)S(1)}, bf16[64]{0:T(256)(128)(2,1)}, u32[]{:S(2)}) copy-start(bf16[64]{0:T(256)(128)(2,1)} %param.21) | copy-start | bytes 388
  7.2 6.8 %copy-start.18 = (bf16[64]{0:T(256)(128)(2,1)S(1)}, bf16[64]{0:T(256)(128)(2,1)}, u32[]{:S(2)}) copy-start(bf16[64]{0:T(256)(128)(2,1)} %param.22) | copy-start | bytes 388
  7.2 34.0 %all-gather.6.cloned.1.call-start = ((), (), s32[]{:S(2)}) async-start(), calls=%async_computation.4 | async-start | bytes 1310720 | tf_op jit(solution)/shard_map/all_gather | solution.py:1195
  8.0 101.7 %all-gather.4.cloned.1.call-start = ((), (), s32[]{:S(2)}) async-start(), calls=%async_computation.3 | async-start | bytes 3932160 | tf_op jit(solution)/shard_map/all_gather | solution.py:1195
  30.2 182.0 %all-gather.8.cloned.1.call-start = ((), (), s32[]{:S(2)}) async-start(), calls=%async_computation.5 | async-start | bytes 7208960 | tf_op jit(solution)/shard_map/all_gather | solution.py:1195
  36.1 84.6 %copy-start.13 = (s32[8]{0:T(128)}, s32[8]{0:T(128)S(1)}, u32[]{:S(2)}) copy-start(s32[8]{0:T(128)S(1)} %get-tuple-element.133.prefix_ref) | copy-start | bytes 100
  106.4 326.3 %reduce-scatter.4.cloned.1.call-start = ((), (), s32[]{:S(2)}) async-start(), calls=%async_computation.6 | async-start | bytes 3604480 | tf_op jit(solution)/shard_map/reduce_scatter | solution.py:1237
  109.6 22.1 %copy-start.5 = (f32[8,2048]{1,0:T(8,128)}, f32[8,2048]{1,0:T(8,128)S(1)}, u32[]{:S(2)}) copy-start(f32[8,2048]{1,0:T(8,128)S(1)} %pad_convert_fusion.refs_2_.gains_ref) | copy-start | bytes 196612
  120.7 11.0 %copy-start.2 = (bf16[224,2048]{1,0:T(8,128)(2,1)S(1)}, bf16[224,2048]{1,0:T(8,128)(2,1)}, u32[]{:S(2)}) copy-start(bf16[224,2048]{1,0:T(8,128)(2,1)} %refs_3_.1) | copy-start | bytes 2752516
  120.7 11.0 %copy-start.7 = (bf16[256,2048]{1,0:T(8,128)(2,1)S(1)}, bf16[256,2048]{1,0:T(8,128)(2,1)}, u32[]{:S(2)}) copy-start(bf16[256,2048]{1,0:T(8,128)(2,1)} %all-gather.6.cloned.1.call-done.refs_1_) | copy-start | bytes 3145732
  131.7 1.2 copy-start
  316.8 160.3 %reduce-scatter.6.cloned.1.call-start = ((), (), s32[]{:S(2)}) async-start(), calls=%async_computation.7 | async-start | bytes 7208960 | tf_op jit(solution)/shard_map/reduce_scatter | solution.py:1198
  347.1 1.5 copy-start.4
  347.1 1.5 copy-start.6
  347.1 209.4 %reduce-scatter.8.cloned.1.call-start = ((), (), s32[]{:S(2)}) async-start(), calls=%async_computation.8 | async-start | bytes 5242880 | tf_op jit(solution)/shard_map/reduce_scatter | solution.py:1198
  348.6 84.1 %copy-start.1 = (bf16[1792,256]{1,0:T(8,128)(2,1)S(1)}, bf16[1792,256]{1,0:T(8,128)(2,1)}, u32[]{:S(2)}) copy-start(bf16[1792,256]{1,0:T(8,128)(2,1)} %get-tuple-element.79) | copy-start | bytes 2752516
  431.4 1.2 copy-start.3
  437.9 1.2 copy-start.8
  469.4 7.7 %copy-start.10 = (bf16[224,2048]{1,0:T(8,128)(2,1)S(1)}, bf16[224,2048]{1,0:T(8,128)(2,1)}, u32[]{:S(2)}) copy-start(bf16[224,2048]{1,0:T(8,128)(2,1)} %get-tuple-element.87) | copy-start | bytes 2752516
  471.7 7.3 %copy-start.11 = (bf16[1,704,512]{2,1,0:T(8,128)(2,1)S(1)}, bf16[1,704,512]{2,1,0:T(8,128)(2,1)}, u32[]{:S(2)}) copy-start(bf16[1,704,512]{2,1,0:T(8,128)(2,1)} %reduce-scatter.4.cloned.1.call-done) | copy-start | bytes 2162692
  574.7 5.0 copy-start.12
  (1 other events, 0.9 us)
Sparse Core Ops, SparseCore 0:
  9.6 30.6 all-gather.5
  41.9 63.0 all-gather.3
  106.5 105.3 all-gather.7
  316.9 55.8 reduce-scatter.3
  374.9 102.1 reduce-scatter.5
  479.2 77.2 reduce-scatter.7
where the time goes:
time: 595 us; the launch traced here: 588 us
  Pallas kernels  476 us (80%)
  matrix products  48.5 us (8%)
  local copies, waits for them, and re-layouts  25.7 us (4%)
  between operations  16.7 us (3%)
  waiting for transfers between devices  11.5 us (2%)
  other arithmetic  8.11 us (1%)
    pallas_call x3, Pallas kernels, group_fold(): pl.pallas_call(functools.partial(fold_kernel, mode, across, zs, width //...  228 us
    pallas_call x1, Pallas kernels, turn(): pl.pallas_call(functools.partial(turn_kernel, zs, width // (8 * zs)), out...  105 us
    pallas_call x1, Pallas kernels, enter(): pl.pallas_call(functools.partial(enter_kernel, zs, kinds), out_shape=[jax...  65.1 us
    dot_general x3, matrix products, dot_rows(): lax.dot_general(left, right, (((0,), (0,)), ((), ())), preferred_element_...  31.3 us
    pallas_call x1, Pallas kernels, closing(): pl.pallas_call(functools.partial(closing_kernel, zs), out_shape=[jax.Shap...  15.9 us
    pallas_call x1, Pallas kernels, group_swap(): pl.pallas_call(functools.partial(swap_kernel, zs, kinds), out_shape=swap_...  15.4 us
    pallas_call x1, Pallas kernels, attend_back(): pl.pallas_call(attend_back_kernel, grid=(rows // SEQ_LEN,), in_specs=[SCA...  15 us
    pallas_call x1, Pallas kernels, ff_backward(): pl.pallas_call(ff_back_kernel, grid=(rows // FF_ROWS,), in_specs=[ff_rows...  13.1 us
  transfers between devices with their start and end apart: 6, of which 2 were waited for; matrix products, arithmetic and copies ran while one was open for 12% of the time, Pallas kernels for 61%

commit v1 on v0

--- a/solution.py
+++ b/solution.py
@@ -5,6 +5,7 @@
 from jax import lax
 from jax.experimental import pallas as pl
 from jax.experimental.pallas import tpu as pltpu
+from jax.experimental.layout import Layout, with_layout_constraint
 from jax.sharding import Mesh
 from jax.sharding import PartitionSpec as P
 
@@ -105,6 +106,7 @@
 TABLE = pl.BlockSpec((1, SEQ_LEN, HEAD), lambda s: (s, 0, 0))
 SCALARS = pl.BlockSpec(memory_space=pltpu.SMEM)
 PARAMS = pltpu.CompilerParams(vmem_limit_bytes=56 * 2**20)
+SMALL = pltpu.CompilerParams(vmem_limit_bytes=24 * 2**20)
 
 
 def attend(prefix, packed, cosine, sine):
@@ -343,9 +345,10 @@
     spread = mode != "last"
     if spread:
         all_ref, refs = refs[0], refs[1:]
-    outs, refs = refs[:n_out], refs[n_out:]
+    out_refs, refs = refs[:n_out], refs[n_out:]
     swap_out, refs = refs[:n_swap], refs[n_swap:]
     aux, refs = refs[:n_aux], refs[n_aux:]
+    outs, refs = refs[:n_out], refs[n_out:]
     left, right, part, got, near_x, near_y, from_x, from_y, block, acc, send, recv, local = refs[:13]
     rows, width = block.shape
     cut = near_x.shape[0]
@@ -446,12 +449,17 @@
     if mode == "back":
         outs[-1][0:1] = jnp.sum(acc[0], axis=0, keepdims=True)
         outs[-1][1:2] = jnp.sum(acc[1], axis=0, keepdims=True)
+    stores = [pltpu.make_async_copy(v, r, local.at[5 + n_aux + k]) for k, (v, r) in enumerate(zip(outs, out_refs))]
+    for store in stores:
+        store.start()
     for copy in sent + [far_x, far_y, plain_x, plain_y, more_x, more_y]:
         copy.wait_send()
     if n_swap:
         swap_finish()
     if spread:
         spread_block(cut, 10, block, all_ref, send, recv, local.at[4])
+    for store in stores:
+        store.wait()
 
 
 def group_fold(name, zs, mode, left, right, gains, aux, out_types, extras=(), kinds=()):
@@ -467,8 +475,8 @@
         functools.partial(fold_kernel, mode, across, zs, width // (8 * zs), n, len(out_types), kinds),
         out_shape=out_shape + swap_shapes(1, extras, kinds),
         in_specs=[ANY, ANY, ROWS] + [ANY] * (n + n_swap),
-        out_specs=[ANY] * spread + [ROWS] * len(out_types) + [ANY] * n_swap,
-        scratch_shapes=[pltpu.VMEM(a.shape, a.dtype) for a in aux]
+        out_specs=[ANY] * (spread + len(out_types) + n_swap),
+        scratch_shapes=[pltpu.VMEM(a.shape, a.dtype) for a in list(aux) + out_types]
         + [
             pltpu.VMEM((4, 2 * rows, depth), BF16),
             pltpu.VMEM(right.shape, BF16),
@@ -482,7 +490,7 @@
             pltpu.VMEM((2, SLAB, width), F32),
             pltpu.SemaphoreType.DMA((n_sems,)),
             pltpu.SemaphoreType.DMA((n_sems,)),
-            pltpu.SemaphoreType.DMA((5 + n,)),
+            pltpu.SemaphoreType.DMA((5 + n + len(out_types),)),
         ]
         + (swap_scratch(1, kinds) if n_swap else []),
         compiler_params=pltpu.CompilerParams(
@@ -494,7 +502,7 @@
 
 def turn_kernel(
     zs, piece, x_ref, in_ref, out_ref, gains_ref, first_ref, grad_ref,
-    all_ref, kept_ref, right_ref, result_ref, d_pre_ref, sums_ref, dw_ref,
+    all_ref, kept_ref, right_ref, result_out, d_pre_out, sums_ref, dw_out, result_ref, d_pre_ref, dw_ref,
     first, grad, w_in, kept, left, right, part, got, near_x, near_y, from_x, from_y, whole, dw, acc,
     fold_send, fold_recv, all_send, all_recv, line_send, line_recv, local, x_local
 ):
@@ -772,11 +780,18 @@
                 dw[block] = found
             elif last:
                 dw_ref[block] = (dw[block] + found).astype(BF16)
+                pltpu.make_async_copy(dw_ref.at[block], dw_out.at[block], x_local.at[block]).start()
             else:
                 dw[block] += found
 
     norm(0)
     norm(1)
+    stores = [
+        pltpu.make_async_copy(result_ref, result_out, local.at[10]),
+        pltpu.make_async_copy(d_pre_ref, d_pre_out, local.at[11]),
+    ]
+    for store in stores:
+        store.start()
     spread_first(0)
     for i in (0, 1):
         landed(alls, 13 * i + 4, whole.at[other, span(i)])
@@ -800,7 +815,9 @@
         landed(alls, 13 * i + 11, whole.at[other_far, low(i)])
         landed(alls, 13 * i + 12, whole.at[other_far, high(i)])
     gradient(0, last=True)
-    for copy in outward + [keep, carry]:
+    for block in range(zs):
+        pltpu.make_async_copy(dw_ref.at[block], dw_out.at[block], x_local.at[block]).wait()
+    for copy in outward + [keep, carry] + stores:
         copy.wait()
     for copy in sent:
         copy.wait_send()
@@ -830,8 +847,11 @@
             jax.ShapeDtypeStruct(by_z, BF16),
         ],
         in_specs=[ANY, ANY, ANY, ROWS, ANY, ANY],
-        out_specs=[ANY] * 3 + [ROWS] * 4,
+        out_specs=[ANY] * 5 + [ROWS, ANY],
         scratch_shapes=[
+            pltpu.VMEM((rows, width), BF16),
+            pltpu.VMEM((rows, width), F32),
+            pltpu.VMEM(by_z, BF16),
             pltpu.VMEM((rows, width), F32),
             pltpu.VMEM((rows, width), BF16),
             pltpu.VMEM(w_in.shape, BF16),
@@ -853,7 +873,7 @@
             pltpu.SemaphoreType.DMA((26,)),
             pltpu.SemaphoreType.DMA((2 * (zs - 1),)),
             pltpu.SemaphoreType.DMA((2 * (zs - 1),)),
-            pltpu.SemaphoreType.DMA((10,)),
+            pltpu.SemaphoreType.DMA((12,)),
             pltpu.SemaphoreType.DMA((8,)),
         ],
         compiler_params=pltpu.CompilerParams(collective_id=1, has_side_effects=True, vmem_limit_bytes=60 * 2**20),
@@ -1001,7 +1021,7 @@
             jax.ShapeDtypeStruct((group, rows, tile), BF16),
         ],
         scratch_shapes=[pltpu.VMEM((16, -(-(ff + group * tile) // 128) * 128), F32)],
-        compiler_params=PARAMS,
+        compiler_params=SMALL,
     )(w_in, w_out)
 
 
@@ -1032,7 +1052,7 @@
         ],
         out_specs=[pl.BlockSpec((16, 2 * ff), lambda i: (i, 0)), pl.BlockSpec((16, ff), lambda i: (i, 0))],
         out_shape=[jax.ShapeDtypeStruct((rows, 2 * ff), F32), jax.ShapeDtypeStruct((rows, ff), F32)],
-        compiler_params=PARAMS,
+        compiler_params=SMALL,
     )(in_blocks, out_blocks)
 
 
@@ -1110,7 +1130,7 @@
             pltpu.SemaphoreType.DMA((zs - 1,)),
             pltpu.SemaphoreType.DMA((zs - 1,)),
         ],
-        compiler_params=pltpu.CompilerParams(collective_id=5, has_side_effects=True, vmem_limit_bytes=56 * 2**20),
+        compiler_params=pltpu.CompilerParams(collective_id=5, has_side_effects=True, vmem_limit_bytes=24 * 2**20),
         cost_estimate=pl.CostEstimate(flops=0, bytes_accessed=50 * 2**20, transcendentals=0),
     )(sums, rows)
 
@@ -1246,7 +1266,7 @@
     d_w_qkv = dot_rows(x_all, d_packed).astype(BF16)
     d_dense = dot_rows(context, d_attn).astype(BF16).reshape(zs, piece, group, width)
     d_dense = jnp.swapaxes(d_dense, 1, 2).reshape(D, width)
-    d_w_qkv = jnp.concatenate([d_w_qkv, d_dense], axis=1)
+    d_w_qkv = with_layout_constraint(jnp.concatenate([d_w_qkv, d_dense], axis=1), Layout((0, 1)))
     sums = jnp.concatenate([sums_one[:2], sums_two[:2], jnp.zeros((4, D), F32)])
     d_packed, d_w_qkv, d_w_in, sums = lax.optimization_barrier((d_packed, d_w_qkv, d_w_in, sums))
     d_w_qkv = scatter(d_w_qkv)

time: 595 us -> 588 us (0.988)
  Pallas kernels: 476 us -> 467 us
  waiting for transfers between devices: 11.5 us -> 19 us
    unnamed x44 -> x54, local copies, waits for them, and re-layouts: 10.7 us -> 12.9 us
  transfers between devices with their start and end apart: 6 -> 6, of which waited for: 2 -> 4; matrix products, arithmetic and copies ran while one was open for 12% -> 11% of each run, Pallas kernels for 61% -> 60%
where the time goes in v1:
time: 588 us; the launch traced here: 581 us
  Pallas kernels  467 us (79%)
  matrix products  45.3 us (8%)
  local copies, waits for them, and re-layouts  23.6 us (4%)
  waiting for transfers between devices  19 us (3%)
  between operations  16.9 us (3%)
  other arithmetic  8.41 us (1%)
    pallas_call x3, Pallas kernels, group_fold(): pl.pallas_call(functools.partial(fold_kernel, mode, across, zs, width //...  227 us
    pallas_call x1, Pallas kernels, turn(): pl.pallas_call(functools.partial(turn_kernel, zs, width // (8 * zs)), out...  103 us
    pallas_call x1, Pallas kernels, enter(): pl.pallas_call(functools.partial(enter_kernel, zs, kinds), out_shape=[jax...  65 us
    dot_general x3, matrix products, dot_rows(): lax.dot_general(left, right, (((0,), (0,)), ((), ())), preferred_element_...  31.5 us
    pallas_call x1, Pallas kernels, group_swap(): pl.pallas_call(functools.partial(swap_kernel, zs, kinds), out_shape=swap_...  15.4 us
    reduce_scatter x2, waiting for transfers between devices, scatter(): lax.psum_scatter(partial.astype(BF16), 'z', scatter_dimension=0, tiled=True)  15.4 us
    pallas_call x1, Pallas kernels, attend_back(): pl.pallas_call(attend_back_kernel, grid=(rows // SEQ_LEN,), in_specs=[SCA...  15 us
    pallas_call x1, Pallas kernels, closing(): pl.pallas_call(functools.partial(closing_kernel, zs), out_shape=[jax.Shap...  13.6 us
  transfers between devices with their start and end apart: 6, of which 4 were waited for; matrix products, arithmetic and copies ran while one was open for 11% of the time, Pallas kernels for 60%

profile of v1, /device:TPU:0, one launch (start us, length us, event | category | flops | bytes accessed | tf_op | source)
XLA Modules:
  0.0 581.1 jit_solution(11332824328721232657)
XLA Ops:
  9.7 1.7 reshape.214.refs_0_
  14.8 15.4 %shard_map.204 = (bf16[8,64,768]{2,1,0:T(8,128)(2,1)}, bf16[8,16,384]{2,1,0:T(8,128)(2,1)}) custom-call(bf16[8,64,768]{2,1,0:T(8,128)(2,1)} %reshape.214.refs_0_, bf16[16,384]{1,0:T(8,128)(2,1)} %pad.15.refs_1_), custom_call_target="tpu_custom_call" | custom-call | bytes 52428800 | tf_op jit(solution)/shard_map/pallas_call | solution.py:892
  35.1 5.0 sine_multiply_fusion
  40.3 65.0 %shard_map.206 = (bf16[8,224,2048]{2,1,0:T(8,128)(2,1)}, bf16[224,2048]{1,0:T(8,128)(2,1)}, bf16[8,64,1408]{2,1,0:T(8,128)(2,1)}, bf16[8,64,704]{2,1,0:T(8,128)(2,1)}, bf16[4,16,384]{2,1,0:T(8,128)(2,1)}) custom-call(bf16[224,2048]{1,0:T(8,128)(2,1)} %refs_3_.1, bf16[224,2048]{1,0:T(8,128)(2,1)} %grad_ref.1, bf16[8,64,1408]{2,1,0:T(8,128)(2,1)} %copy-done.7, ...), custom_call_target="tpu_custom_call" | custom-call | bytes 157286400 | tf_op jit(solution)/shard_map/pallas_call | solution.py:923
  106.3 2.3 copy.34
  108.6 10.7 %fusion.4.packed_ref = f32[1792,768]{1,0:T(8,128)} fusion(bf16[1792,2048]{1,0:T(8,128)(2,1)} %bitcast.85, bf16[2048,768]{1,0:T(8,128)(2,1)} %all-gather.4.cloned.1.call-done.refs_1_), kind=kOutput, calls=%fused_computation.31 | convolution fusion | flops 5637144576 | bytes 15990784 | tf_op jit(solution)/shard_map/dot_general | solution.py:29
  119.3 11.0 %shard_map.207 = (bf16[1792,768]{1,0:T(8,128)(2,1)}, bf16[1792,256]{1,0:T(8,128)(2,1)}) custom-call(s32[8]{0:T(128)} %copy-done.18, f32[1792,768]{1,0:T(8,128)} %fusion.4.packed_ref, f32[8,224,128]{2,1,0:T(8,128)} %get-tuple-element.77.cos_ref, f32[8,224,128]{2,1,0:T(8,128)} %get-tuple-element.78.sin_ref), custom_call_target="tpu_custom_call" | custom-call | tf_op jit(solution)/shard_map/pallas_call | solution.py:114
  131.5 77.8 %shard_map.208 = (bf16[8,224,2048]{2,1,0:T(8,128)(2,1)}, f32[224,2048]{1,0:T(8,128)}, f32[224,2048]{1,0:T(8,128)}, f32[224,128]{1,0:T(8,128)S(1)}) custom-call(bf16[4,448,256]{2,1,0:T(8,128)(2,1)S(1)} %bitcast.60, bf16[256,2048]{1,0:T(8,128)(2,1)S(1)} %copy-done.10, f32[8,2048]{1,0:T(8,128)S(1)} %pad_convert_fusion.refs_2_.gains_ref, ...), custom_call_target="tpu_custom_call" | custom-call | bytes 209715200 | tf_op jit(solution)/shard_map/pallas_call | solution.py:474
  209.3 2.7 all-gather.8.cloned.1.call-done.in_ref.refs_1_
  211.9 103.1 %shard_map.209 = (bf16[8,224,2048]{2,1,0:T(8,128)(2,1)}, bf16[8,224,1408]{2,1,0:T(8,128)(2,1)}, bf16[4,704,512]{2,1,0:T(8,128)(2,1)}, bf16[224,2048]{1,0:T(8,128...) custom-call(bf16[8,224,2048]{2,1,0:T(8,128)(2,1)} %get-tuple-element.82.x_ref, ...), custom_call_target="tpu_custom_call" | custom-call | bytes 398458880 | tf_op jit(solution)/shard_map/pallas_call | solution.py:838
  315.3 13.0 %shard_map.210 = bf16[1792,1408]{1,0:T(8,128)(2,1)} custom-call(bf16[1792,2048]{1,0:T(8,128)(2,1)} %bitcast.68, bf16[4,704,512]{2,1,0:T(8,128)(2,1)} %get-tuple-element.90.w_ref, bf16[1792,1408]{1,0:T(8,128)(2,1)} %bitcast.69), custom_call_target="tpu_custom_call" | custom-call | flops 5167382528 | bytes 20971520 | tf_op jit(solution)/shard_map/pallas_call | solution.py:978
  328.3 17.0 %convolution_convert_fusion = bf16[2048,1408]{1,0:T(8,128)(2,1)} fusion(bf16[1792,2048]{1,0:T(8,128)(2,1)} %bitcast.67, bf16[1792,1408]{1,0:T(8,128)(2,1)} %shard_map.210), kind=kOutput, calls=%fused_computation | convolution fusion | flops 10337648640 | bytes 18153472 | tf_op jit(solution)/shard_map/dot_general | solution.py:33
  346.9 83.3 %shard_map.211 = (bf16[8,224,2048]{2,1,0:T(8,128)(2,1)}, f32[224,2048]{1,0:T(8,128)S(1)}, f32[8,2048]{1,0:T(8,128)S(1)}) custom-call(bf16[4,448,1408]{2,1,0:T(8,128)(2,1)} %bitcast.65, bf16[2048,1408]{1,0:T(8,128)(2,1)} %all-gather.8.cloned.1.call-done.in_ref.refs_1_, f32[8,2048]{1,0:T(8,128)S(1)} %copy-done.6, f32[224,2048]{1,0:T(8,128)S(1)} %copy-done.4, ...), custom_call_target="tpu_custom_call" | custom-call | bytes 209715200 | tf_op jit(solution)/shard_map/pallas_call | solution.py:474
  431.6 5.3 convolution_convert_fusion.2
  437.5 3.2 convolution_convert_fusion.3.d_context_ref
  440.7 15.0 %shard_map.212 = bf16[1792,768]{1,0:T(8,128)(2,1)} custom-call(s32[8]{0:T(128)} %copy-done.18, bf16[1792,768]{1,0:T(8,128)(2,1)} %get-tuple-element.88.qkv_ref, bf16[1792,256]{1,0:T(8,128)(2,1)} %convolution_convert_fusion.3.d_context_ref, f32[8,224,128]{2,1,0:T(8,128)} %get-tuple-element.77.cos_ref, f32[8,224,128]{2,1,0:T(8,128)} %get-tuple-element.78.sin_ref), custom_call_target="tpu_custom_call" | custom-call | tf_op jit(solution)/shard_map/pallas_call | solution.py:129
  455.8 9.1 %convolution_convert_fusion.1 = bf16[2048,768]{1,0:T(8,128)(2,1)S(1)} fusion(bf16[1792,2048]{1,0:T(8,128)(2,1)} %bitcast.86, bf16[1792,768]{1,0:T(8,128)(2,1)} %shard_map.212), kind=kOutput, calls=%fused_computation.2 | convolution fusion | flops 5638717440 | bytes 13238272 | tf_op jit(solution)/shard_map/dot_general | solution.py:33
  464.9 2.6 pad_maximum_fusion
  467.4 8.6 %reduce-scatter.6.cloned.1.call-done = bf16[512,1408]{1,0:T(8,128)(2,1)} async-done(((bf16[2048,1408]{1,0:T(8,128)(2,1)}), bf16[512,1408]{1,0:T(8,128)(2,1)}) %reduce-scatter.6.cloned.1.call-update) | async-done | bytes 1441808 | tf_op jit(solution)/shard_map/reduce_scatter | solution.py:1218
  478.3 66.0 %shard_map.213 = (bf16[224,2048]{1,0:T(8,128)(2,1)S(1)}, bf16[8,64,1408]{2,1,0:T(8,128)(2,1)}, bf16[8,64,704]{2,1,0:T(8,128)(2,1)S(1)}, f32[8,8,2048]{2,1,0:T(8,128)S(1)}) custom-call(bf16[4,448,768]{2,1,0:T(8,128)(2,1)} %bitcast.66, bf16[2048,768]{1,0:T(8,128)(2,1)} %all-gather.4.cloned.1.call-done.refs_1_, f32[8,2048]{1,0:T(8,128)S(1)} %copy-done.6, ...), custom_call_target="tpu_custom_call" | custom-call | bytes 115343360 | tf_op jit(solution)/shard_map/pallas_call | solution.py:474
  544.5 1.4 copy-done.8
  545.9 2.8 shard_map.214
  548.7 6.8 %reduce-scatter.8.cloned.1.call-done = bf16[512,1024]{1,0:T(8,128)(2,1)} async-done(((bf16[2048,1024]{1,0:T(8,128)(2,1)}), bf16[512,1024]{1,0:T(8,128)(2,1)}) %reduce-scatter.8.cloned.1.call-update) | async-done | bytes 1048592 | tf_op jit(solution)/shard_map/reduce_scatter | solution.py:1218
  556.7 13.6 %shard_map.215 = (f32[64,6144]{1,0:T(8,128)S(1)}, f32[64,2048]{1,0:T(8,128)S(1)}, f32[8,64]{1,0:T(8,128)S(1)}) custom-call(f32[8,256]{1,0:T(8,128)S(1)} %reshape.235.sum_ref, bf16[8,64,1024]{2,1,0:T(8,128)(2,1)S(1)} %bitcast.62), custom_call_target="tpu_custom_call" | custom-call | bytes 52428800 | tf_op jit(solution)/shard_map/pallas_call | solution.py:1114
  (101 shorter events, 21.8 us)
Async XLA Ops:
  7.2 4.9 copy-start.19
  7.2 6.8 %copy-start.20 = (bf16[64]{0:T(256)(128)(2,1)S(1)}, bf16[64]{0:T(256)(128)(2,1)}, u32[]{:S(2)}) copy-start(bf16[64]{0:T(256)(128)(2,1)} %param.19) | copy-start | bytes 388
  7.2 6.8 %copy-start.21 = (bf16[64]{0:T(256)(128)(2,1)S(1)}, bf16[64]{0:T(256)(128)(2,1)}, u32[]{:S(2)}) copy-start(bf16[64]{0:T(256)(128)(2,1)} %param.20) | copy-start | bytes 388
  7.2 6.8 %copy-start.22 = (bf16[64]{0:T(256)(128)(2,1)S(1)}, bf16[64]{0:T(256)(128)(2,1)}, u32[]{:S(2)}) copy-start(bf16[64]{0:T(256)(128)(2,1)} %param.21) | copy-start | bytes 388
  7.2 6.8 %copy-start.23 = (bf16[64]{0:T(256)(128)(2,1)S(1)}, bf16[64]{0:T(256)(128)(2,1)}, u32[]{:S(2)}) copy-start(bf16[64]{0:T(256)(128)(2,1)} %param.22) | copy-start | bytes 388
  7.2 24.6 %copy-start.9 = (bf16[64,10922]{1,0:T(8,128)(2,1)S(1)}, bf16[64,10922]{1,0:T(8,128)(2,1)}, u32[]{:S(2)}) copy-start(bf16[64,10922]{1,0:T(8,128)(2,1)} %in_ref.1) | copy-start | bytes 4194052
  7.2 24.6 %copy-start.14 = (bf16[64,5461]{1,0:T(8,128)(2,1)S(1)}, bf16[64,5461]{1,0:T(8,128)(2,1)}, u32[]{:S(2)}) copy-start(bf16[64,5461]{1,0:T(8,128)(2,1)} %out_ref.1) | copy-start | bytes 2097028
  7.2 33.1 %all-gather.6.cloned.1.call-start = ((), (), s32[]{:S(2)}) async-start(), calls=%async_computation.4 | async-start | bytes 1310720 | tf_op jit(solution)/shard_map/all_gather | solution.py:1215
  8.0 100.6 %all-gather.4.cloned.1.call-start = ((), (), s32[]{:S(2)}) async-start(), calls=%async_computation.3 | async-start | bytes 3932160 | tf_op jit(solution)/shard_map/all_gather | solution.py:1215
  30.3 181.7 %all-gather.8.cloned.1.call-start = ((), (), s32[]{:S(2)}) async-start(), calls=%async_computation.5 | async-start | bytes 7208960 | tf_op jit(solution)/shard_map/all_gather | solution.py:1215
  35.1 84.2 %copy-start.18 = (s32[8]{0:T(128)}, s32[8]{0:T(128)S(1)}, u32[]{:S(2)}) copy-start(s32[8]{0:T(128)S(1)} %get-tuple-element.133.prefix_ref) | copy-start | bytes 100
  105.3 326.3 %reduce-scatter.4.cloned.1.call-start = ((), (), s32[]{:S(2)}) async-start(), calls=%async_computation.6 | async-start | bytes 3604480 | tf_op jit(solution)/shard_map/reduce_scatter | solution.py:1257
  108.6 21.7 %copy-start.5 = (f32[8,2048]{1,0:T(8,128)}, f32[8,2048]{1,0:T(8,128)S(1)}, u32[]{:S(2)}) copy-start(f32[8,2048]{1,0:T(8,128)S(1)} %pad_convert_fusion.refs_2_.gains_ref) | copy-start | bytes 196612
  119.3 11.0 %copy-start.2 = (bf16[224,2048]{1,0:T(8,128)(2,1)S(1)}, bf16[224,2048]{1,0:T(8,128)(2,1)}, u32[]{:S(2)}) copy-start(bf16[224,2048]{1,0:T(8,128)(2,1)} %refs_3_.1) | copy-start | bytes 2752516
  119.3 11.0 %copy-start.10 = (bf16[256,2048]{1,0:T(8,128)(2,1)S(1)}, bf16[256,2048]{1,0:T(8,128)(2,1)}, u32[]{:S(2)}) copy-start(bf16[256,2048]{1,0:T(8,128)(2,1)} %all-gather.6.cloned.1.call-done.refs_1_) | copy-start | bytes 3145732
  315.1 161.0 %reduce-scatter.6.cloned.1.call-start = ((), (), s32[]{:S(2)}) async-start(), calls=%async_computation.7 | async-start | bytes 7208960 | tf_op jit(solution)/shard_map/reduce_scatter | solution.py:1218
  345.4 1.5 copy-start.4
  345.4 1.5 copy-start.6
  345.4 210.1 %reduce-scatter.8.cloned.1.call-start = ((), (), s32[]{:S(2)}) async-start(), calls=%async_computation.8 | async-start | bytes 5242880 | tf_op jit(solution)/shard_map/reduce_scatter | solution.py:1218
  346.9 84.7 %copy-start.1 = (bf16[1792,256]{1,0:T(8,128)(2,1)S(1)}, bf16[1792,256]{1,0:T(8,128)(2,1)}, u32[]{:S(2)}) copy-start(bf16[1792,256]{1,0:T(8,128)(2,1)} %get-tuple-element.79) | copy-start | bytes 2752516
  431.6 5.9 %copy-start.11 = (bf16[256,2048]{1,0:T(8,128)(2,1)S(1)}, bf16[256,2048]{1,0:T(8,128)(2,1)}, u32[]{:S(2)}) copy-start(bf16[256,2048]{1,0:T(8,128)(2,1)} %all-gather.6.cloned.1.call-done.refs_1_) | copy-start | bytes 3145732
  431.6 5.9 %copy-start.15 = (bf16[8,224,2048]{2,1,0:T(8,128)(2,1)S(1)}, bf16[8,224,2048]{2,1,0:T(8,128)(2,1)}, u32[]{:S(2)}) copy-start(bf16[8,224,2048]{2,1,0:T(8,128)(2,1)} %get-tuple-element.96) | copy-start | bytes 22020100
  464.9 11.2 %copy-start.16 = (bf16[224,2048]{1,0:T(8,128)(2,1)S(1)}, bf16[224,2048]{1,0:T(8,128)(2,1)}, u32[]{:S(2)}) copy-start(bf16[224,2048]{1,0:T(8,128)(2,1)} %get-tuple-element.87) | copy-start | bytes 2752516
  467.4 10.6 %copy-start.17 = (bf16[1,704,512]{2,1,0:T(8,128)(2,1)S(1)}, bf16[1,704,512]{2,1,0:T(8,128)(2,1)}, u32[]{:S(2)}) copy-start(bf16[1,704,512]{2,1,0:T(8,128)(2,1)} %reduce-scatter.4.cloned.1.call-done) | copy-start | bytes 2162692
  (6 other events, 7.0 us)
Sparse Core Ops, SparseCore 0:
  9.7 30.6 all-gather.5
  41.9 62.9 all-gather.3
  106.5 105.3 all-gather.7
  315.2 56.5 reduce-scatter.3
  373.9 102.0 reduce-scatter.5
  478.2 77.2 reduce-scatter.7

commit v2 on v1

--- a/solution.py
+++ b/solution.py
@@ -1056,7 +1056,7 @@
     )(in_blocks, out_blocks)
 
 
-def closing_kernel(zs, sum_ref, rows_ref, qkv_ref, dense_ref, total_ref, got, mine, lines, *refs):
+def closing_kernel(zs, sum_ref, rows_ref, qkv_ref, total_ref, got, lines, *refs):
     send, recv, local, line_send, line_recv = refs
     y, x, c = here()
     z = lax.axis_index("z")
@@ -1069,8 +1069,7 @@
     copies, comes = [], []
     for k, (peer, name) in enumerate(found[:7]):
         sems = dict(send_sem=send.at[k], recv_sem=recv.at[k], device_id=name, device_id_type=MESH)
-        src = rows_ref.at[peer, :, pl.ds(0, wide)]
-        copies.append(pltpu.make_async_remote_copy(src_ref=src, dst_ref=got.at[me], **sems))
+        copies.append(pltpu.make_async_remote_copy(src_ref=rows_ref.at[peer], dst_ref=got.at[me], **sems))
         comes.append(pltpu.make_async_remote_copy(src_ref=got.at[peer], dst_ref=got.at[peer], **sems))
     for k, (peer, name) in enumerate(found[7:]):
         sems = dict(send_sem=line_send.at[k], recv_sem=line_recv.at[k], device_id=name, device_id_type=MESH)
@@ -1079,19 +1078,14 @@
     for copy in copies:
         copy.start()
     keeps = [
-        pltpu.make_async_copy(rows_ref.at[me, :, pl.ds(0, wide)], got.at[me], local.at[0]),
+        pltpu.make_async_copy(rows_ref.at[me], got.at[me], local.at[0]),
         pltpu.make_async_copy(sum_ref, lines.at[z], local.at[1]),
-        pltpu.make_async_copy(rows_ref.at[:, :, pl.ds(wide, width)], mine, local.at[2]),
     ]
     for keep in keeps:
         keep.start()
-    keeps[2].wait()
-    for at in range(0, piece, 16):
-        rows = jnp.concatenate([mine[g, at : at + 16] for g in range(8)], axis=1).astype(F32)
-        dense_ref[at : at + 16] = rows
     for come in comes:
         come.wait_recv()
-    for keep in keeps[:2]:
+    for keep in keeps:
         keep.wait()
     for g in range(8):
         for j in range(3):
@@ -1110,23 +1104,21 @@
 
 def closing(zs, sums, rows):
     _, piece, columns = rows.shape
-    width = columns // 4
+    width = columns // 3
     return pl.pallas_call(
         functools.partial(closing_kernel, zs),
         out_shape=[
             jax.ShapeDtypeStruct((piece, 3 * D), F32),
-            jax.ShapeDtypeStruct((piece, D), F32),
             jax.ShapeDtypeStruct((8, piece), F32),
         ],
         in_specs=[ROWS, ANY],
-        out_specs=[ROWS] * 3,
+        out_specs=[ROWS] * 2,
         scratch_shapes=[
             pltpu.VMEM((8, piece, 3 * width), BF16),
-            pltpu.VMEM((8, piece, width), BF16),
             pltpu.VMEM((zs, 8, width), F32),
             pltpu.SemaphoreType.DMA((7,)),
             pltpu.SemaphoreType.DMA((7,)),
-            pltpu.SemaphoreType.DMA((3,)),
+            pltpu.SemaphoreType.DMA((2,)),
             pltpu.SemaphoreType.DMA((zs - 1,)),
             pltpu.SemaphoreType.DMA((zs - 1,)),
         ],
@@ -1264,12 +1256,13 @@
     d_context = dot_cols(d_attn, w_dense_part).astype(BF16)
     d_packed = attend_back(prefix, qkv, d_context, cosine, sine)
     d_w_qkv = dot_rows(x_all, d_packed).astype(BF16)
-    d_dense = dot_rows(context, d_attn).astype(BF16).reshape(zs, piece, group, width)
-    d_dense = jnp.swapaxes(d_dense, 1, 2).reshape(D, width)
-    d_w_qkv = with_layout_constraint(jnp.concatenate([d_w_qkv, d_dense], axis=1), Layout((0, 1)))
     sums = jnp.concatenate([sums_one[:2], sums_two[:2], jnp.zeros((4, D), F32)])
-    d_packed, d_w_qkv, d_w_in, sums = lax.optimization_barrier((d_packed, d_w_qkv, d_w_in, sums))
+    d_w_qkv = with_layout_constraint(d_w_qkv, Layout((0, 1)))
+    d_packed, d_w_qkv, d_w_in, sums, d_attn = lax.optimization_barrier((d_packed, d_w_qkv, d_w_in, sums, d_attn))
     d_w_qkv = scatter(d_w_qkv)
+    d_dense = dot_rows(context, d_attn).astype(BF16)
+    d_dense, d_packed = lax.optimization_barrier((d_dense, d_packed))
+    d_dense = scatter(d_dense)
     d_w_in, d_w_out = d_w_in.reshape(group, piece, 2 * tile), d_w_out.T.reshape(group, piece, tile)
     d_input, d_w_in, d_w_out, sums = fold_last(
         d_packed, w_qkv_part, d_pre_one, gains, [d_w_in, d_w_out, sums], ("swap", "swap", "group")
@@ -1279,16 +1272,15 @@
     out_in, out_out = join_ff(d_w_in, d_w_out, ff)
     out_in, out_out, d_input, d_w_qkv, sums = lax.optimization_barrier((out_in, out_out, d_input, d_w_qkv, sums))
     if own:
-        out_qkv, out_dense, sums = closing(zs, sums, d_w_qkv.reshape(group, piece, 4 * width))
+        out_qkv, sums = closing(zs, sums, d_w_qkv.reshape(group, piece, 3 * width))
     else:
-        out_dense = d_w_qkv[:, 3 * width :].reshape(group, piece, width)
-        out_dense = jnp.swapaxes(out_dense, 0, 1).reshape(piece, D).astype(F32)
-        d_w_qkv = d_w_qkv[:, : 3 * width].reshape(group, piece, 3 * width)
-        d_w_qkv, sums = swap(5, [d_w_qkv, sums], ("swap", "line"))
+        d_w_qkv, sums = swap(5, [d_w_qkv.reshape(group, piece, 3 * width), sums], ("swap", "line"))
         out_qkv = jnp.transpose(d_w_qkv.astype(F32).reshape(group, piece, 3, width), (1, 2, 0, 3))
         out_qkv = out_qkv.reshape(piece, 3 * D)
         sums = jnp.sum(sums, axis=0).reshape(8, zs, piece)
         sums = lax.dynamic_index_in_dim(sums, lax.axis_index("z"), 1, keepdims=False)
+    out_qkv, sums, d_dense = lax.optimization_barrier((out_qkv, sums, d_dense))
+    out_dense = d_dense.astype(F32)
     return layer_out, d_input, out_qkv, out_dense, out_in, out_out, sums[0], sums[1], sums[2], sums[3]
 
 

time: 588 us -> 588 us (level)
    reduce_scatter x2 -> x3, waiting for transfers between devices: 15.4 us -> 13.6 us  [scatter(): lax.psum_scatter(partial.astype(BF16), 'z', scatter_dimension=0, tiled=True)]
    unnamed x54 -> x48, local copies, waits for them, and re-layouts: 12.9 us -> 11.7 us
  transfers between devices with their start and end apart: 6 -> 7, of which waited for: 4 -> 4; matrix products, arithmetic and copies ran while one was open for 11% -> 12% of each run, Pallas kernels for 60% -> 62%
where the time goes in v2:
time: 588 us; the launch traced here: 581 us
  Pallas kernels  466 us (79%)
  matrix products  50.3 us (9%)
  local copies, waits for them, and re-layouts  22.1 us (4%)
  waiting for transfers between devices  17.3 us (3%)
  between operations  16.7 us (3%)
  other arithmetic  7.63 us (1%)
    pallas_call x3, Pallas kernels, group_fold(): pl.pallas_call(functools.partial(fold_kernel, mode, across, zs, width //...  227 us
    pallas_call x1, Pallas kernels, turn(): pl.pallas_call(functools.partial(turn_kernel, zs, width // (8 * zs)), out...  103 us
    pallas_call x1, Pallas kernels, enter(): pl.pallas_call(functools.partial(enter_kernel, zs, kinds), out_shape=[jax...  65 us
    dot_general x3, matrix products, dot_rows(): lax.dot_general(left, right, (((0,), (0,)), ((), ())), preferred_element_...  33.5 us
    pallas_call x1, Pallas kernels, group_swap(): pl.pallas_call(functools.partial(swap_kernel, zs, kinds), out_shape=swap_...  15.4 us
    pallas_call x1, Pallas kernels, attend_back(): pl.pallas_call(attend_back_kernel, grid=(rows // SEQ_LEN,), in_specs=[SCA...  15 us
    reduce_scatter x3, waiting for transfers between devices, scatter(): lax.psum_scatter(partial.astype(BF16), 'z', scatter_dimension=0, tiled=True)  13.6 us
    pallas_call x1, Pallas kernels, ff_backward(): pl.pallas_call(ff_back_kernel, grid=(rows // FF_ROWS,), in_specs=[ff_rows...  13.1 us
  transfers between devices with their start and end apart: 7, of which 4 were waited for; matrix products, arithmetic and copies ran while one was open for 12% of the time, Pallas kernels for 62%

profile of v2, /device:TPU:0, one launch (start us, length us, event | category | flops | bytes accessed | tf_op | source)
XLA Modules:
  0.0 581.1 jit_solution(9464787618499675655)
XLA Ops:
  8.0 1.3 copy.37
  9.7 1.7 reshape.208.refs_0_
  14.8 15.4 %shard_map.204 = (bf16[8,64,768]{2,1,0:T(8,128)(2,1)}, bf16[8,16,384]{2,1,0:T(8,128)(2,1)}) custom-call(bf16[8,64,768]{2,1,0:T(8,128)(2,1)} %reshape.208.refs_0_, bf16[16,384]{1,0:T(8,128)(2,1)} %pad.15.refs_1_), custom_call_target="tpu_custom_call" | custom-call | bytes 52428800 | tf_op jit(solution)/shard_map/pallas_call | solution.py:892
  35.1 5.0 sine_multiply_fusion
  40.3 65.0 %shard_map.206 = (bf16[8,224,2048]{2,1,0:T(8,128)(2,1)}, bf16[224,2048]{1,0:T(8,128)(2,1)}, bf16[8,64,1408]{2,1,0:T(8,128)(2,1)}, bf16[8,64,704]{2,1,0:T(8,128)(2,1)}, bf16[4,16,384]{2,1,0:T(8,128)(2,1)}) custom-call(bf16[224,2048]{1,0:T(8,128)(2,1)} %refs_3_.1, bf16[224,2048]{1,0:T(8,128)(2,1)} %grad_ref.1, bf16[8,64,1408]{2,1,0:T(8,128)(2,1)} %copy-done.7, ...), custom_call_target="tpu_custom_call" | custom-call | bytes 157286400 | tf_op jit(solution)/shard_map/pallas_call | solution.py:923
  106.3 2.3 copy.32
  108.6 10.7 %fusion.4.packed_ref = f32[1792,768]{1,0:T(8,128)} fusion(bf16[1792,2048]{1,0:T(8,128)(2,1)} %bitcast.76, bf16[2048,768]{1,0:T(8,128)(2,1)} %all-gather.4.cloned.1.call-done.refs_1_), kind=kOutput, calls=%fused_computation.30 | convolution fusion | flops 5637144576 | bytes 15990784 | tf_op jit(solution)/shard_map/dot_general | solution.py:29
  119.3 11.0 %shard_map.207 = (bf16[1792,768]{1,0:T(8,128)(2,1)}, bf16[1792,256]{1,0:T(8,128)(2,1)}) custom-call(s32[8]{0:T(128)} %copy-done.16, f32[1792,768]{1,0:T(8,128)} %fusion.4.packed_ref, f32[8,224,128]{2,1,0:T(8,128)} %get-tuple-element.82.cos_ref, f32[8,224,128]{2,1,0:T(8,128)} %get-tuple-element.83.sin_ref), custom_call_target="tpu_custom_call" | custom-call | tf_op jit(solution)/shard_map/pallas_call | solution.py:114
  131.5 77.8 %shard_map.208 = (bf16[8,224,2048]{2,1,0:T(8,128)(2,1)}, f32[224,2048]{1,0:T(8,128)}, f32[224,2048]{1,0:T(8,128)}, f32[224,128]{1,0:T(8,128)S(1)}) custom-call(bf16[4,448,256]{2,1,0:T(8,128)(2,1)S(1)} %bitcast.54, bf16[256,2048]{1,0:T(8,128)(2,1)S(1)} %copy-done.10, f32[8,2048]{1,0:T(8,128)S(1)} %pad_convert_fusion.refs_2_.gains_ref, ...), custom_call_target="tpu_custom_call" | custom-call | bytes 209715200 | tf_op jit(solution)/shard_map/pallas_call | solution.py:474
  209.2 2.7 all-gather.8.cloned.1.call-done.in_ref.refs_1_
  211.9 103.3 %shard_map.209 = (bf16[8,224,2048]{2,1,0:T(8,128)(2,1)}, bf16[8,224,1408]{2,1,0:T(8,128)(2,1)}, bf16[4,704,512]{2,1,0:T(8,128)(2,1)}, bf16[224,2048]{1,0:T(8,128...) custom-call(bf16[8,224,2048]{2,1,0:T(8,128)(2,1)} %get-tuple-element.87.x_ref, ...), custom_call_target="tpu_custom_call" | custom-call | bytes 398458880 | tf_op jit(solution)/shard_map/pallas_call | solution.py:838
  315.5 13.1 %shard_map.210 = bf16[1792,1408]{1,0:T(8,128)(2,1)} custom-call(bf16[1792,2048]{1,0:T(8,128)(2,1)} %bitcast.62, bf16[4,704,512]{2,1,0:T(8,128)(2,1)} %get-tuple-element.95.w_ref, bf16[1792,1408]{1,0:T(8,128)(2,1)} %bitcast.63), custom_call_target="tpu_custom_call" | custom-call | flops 5167382528 | bytes 20971520 | tf_op jit(solution)/shard_map/pallas_call | solution.py:978
  328.6 17.0 %convolution_convert_fusion = bf16[2048,1408]{1,0:T(8,128)(2,1)} fusion(bf16[1792,2048]{1,0:T(8,128)(2,1)} %bitcast.61, bf16[1792,1408]{1,0:T(8,128)(2,1)} %shard_map.210), kind=kOutput, calls=%fused_computation | convolution fusion | flops 10337648640 | bytes 18153472 | tf_op jit(solution)/shard_map/dot_general | solution.py:33
  347.1 83.2 %shard_map.211 = (bf16[8,224,2048]{2,1,0:T(8,128)(2,1)}, f32[224,2048]{1,0:T(8,128)S(1)}, f32[8,2048]{1,0:T(8,128)S(1)}) custom-call(bf16[4,448,1408]{2,1,0:T(8,128)(2,1)} %bitcast.59, bf16[2048,1408]{1,0:T(8,128)(2,1)} %all-gather.8.cloned.1.call-done.in_ref.refs_1_, f32[8,2048]{1,0:T(8,128)S(1)} %copy-done.6, f32[224,2048]{1,0:T(8,128)S(1)} %copy-done.4, ...), custom_call_target="tpu_custom_call" | custom-call | bytes 209715200 | tf_op jit(solution)/shard_map/pallas_call | solution.py:474
  431.7 6.1 %convolution_convert_fusion.3.d_context_ref = bf16[1792,256]{1,0:T(8,128)(2,1)} fusion(bf16[1792,2048]{1,0:T(8,128)(2,1)} %bitcast.57, bf16[256,2048]{1,0:T(8,128)(2,1)S(1)} %copy-done.10), kind=kOutput, calls=%fused_computation.3 | convolution fusion | flops 1879506944 | bytes 9306112 | tf_op jit(solution)/shard_map/dot_general | solution.py:37
  437.8 15.0 %shard_map.212 = bf16[1792,768]{1,0:T(8,128)(2,1)} custom-call(s32[8]{0:T(128)} %copy-done.16, bf16[1792,768]{1,0:T(8,128)(2,1)} %get-tuple-element.93.qkv_ref, bf16[1792,256]{1,0:T(8,128)(2,1)} %convolution_convert_fusion.3.d_context_ref, f32[8,224,128]{2,1,0:T(8,128)} %get-tuple-element.82.cos_ref, f32[8,224,128]{2,1,0:T(8,128)} %get-tuple-element.83.sin_ref), custom_call_target="tpu_custom_call" | custom-call | tf_op jit(solution)/shard_map/pallas_call | solution.py:129
  452.8 10.4 %convolution_convert_fusion.1 = bf16[2048,768]{1,0:T(8,128)(2,1)} fusion(bf16[1792,2048]{1,0:T(8,128)(2,1)} %bitcast.77, bf16[1792,768]{1,0:T(8,128)(2,1)} %shard_map.212), kind=kOutput, calls=%fused_computation.1 | convolution fusion | flops 5638717440 | bytes 13238272 | tf_op jit(solution)/shard_map/dot_general | solution.py:33
  463.2 12.8 %reduce-scatter.7.cloned.1.call-done = bf16[512,1408]{1,0:T(8,128)(2,1)} async-done(((bf16[2048,1408]{1,0:T(8,128)(2,1)}), bf16[512,1408]{1,0:T(8,128)(2,1)}) %reduce-scatter.7.cloned.1.call-update) | async-done | bytes 1441808 | tf_op jit(solution)/shard_map/reduce_scatter | solution.py:1210
  476.4 6.1 %convolution_convert_fusion.2 = bf16[256,2048]{1,0:T(8,128)(2,1)} fusion(bf16[1792,256]{1,0:T(8,128)(2,1)S(1)} %copy-done.1, bf16[1792,2048]{1,0:T(8,128)(2,1)} %bitcast.58), kind=kOutput, calls=%fused_computation.2 | convolution fusion | flops 1879572480 | bytes 9306112 | tf_op jit(solution)/shard_map/dot_general | solution.py:33
  484.7 66.0 %shard_map.213 = (bf16[224,2048]{1,0:T(8,128)(2,1)S(1)}, bf16[8,64,1408]{2,1,0:T(8,128)(2,1)}, bf16[8,64,704]{2,1,0:T(8,128)(2,1)S(1)}, f32[8,8,2048]{2,1,0:T(8,128)S(1)}) custom-call(bf16[4,448,768]{2,1,0:T(8,128)(2,1)} %bitcast.60, bf16[2048,768]{1,0:T(8,128)(2,1)} %all-gather.4.cloned.1.call-done.refs_1_, f32[8,2048]{1,0:T(8,128)S(1)} %copy-done.6, ...), custom_call_target="tpu_custom_call" | custom-call | bytes 115343360 | tf_op jit(solution)/shard_map/pallas_call | solution.py:474
  551.0 1.4 copy-done.8
  552.4 2.8 shard_map.214
  556.3 12.5 %shard_map.215 = (f32[64,6144]{1,0:T(8,128)S(1)}, f32[8,64]{1,0:T(8,128)S(1)}) custom-call(f32[8,256]{1,0:T(8,128)S(1)} %reshape.227.sum_ref, bf16[8,64,768]{2,1,0:T(8,128)(2,1)S(1)} %bitcast.56), custom_call_target="tpu_custom_call" | custom-call | bytes 52428800 | tf_op jit(solution)/shard_map/pallas_call | solution.py:1108
  569.6 1.8 convert_element_type.43
  (97 shorter events, 20.0 us)
Async XLA Ops:
  7.2 4.9 copy-start.17
  7.2 6.8 %copy-start.18 = (bf16[64]{0:T(256)(128)(2,1)S(1)}, bf16[64]{0:T(256)(128)(2,1)}, u32[]{:S(2)}) copy-start(bf16[64]{0:T(256)(128)(2,1)} %param.19) | copy-start | bytes 388
  7.2 6.8 %copy-start.19 = (bf16[64]{0:T(256)(128)(2,1)S(1)}, bf16[64]{0:T(256)(128)(2,1)}, u32[]{:S(2)}) copy-start(bf16[64]{0:T(256)(128)(2,1)} %param.20) | copy-start | bytes 388
  7.2 6.8 %copy-start.20 = (bf16[64]{0:T(256)(128)(2,1)S(1)}, bf16[64]{0:T(256)(128)(2,1)}, u32[]{:S(2)}) copy-start(bf16[64]{0:T(256)(128)(2,1)} %param.21) | copy-start | bytes 388
  7.2 6.8 %copy-start.21 = (bf16[64]{0:T(256)(128)(2,1)S(1)}, bf16[64]{0:T(256)(128)(2,1)}, u32[]{:S(2)}) copy-start(bf16[64]{0:T(256)(128)(2,1)} %param.22) | copy-start | bytes 388
  7.2 24.6 %copy-start.9 = (bf16[64,10922]{1,0:T(8,128)(2,1)S(1)}, bf16[64,10922]{1,0:T(8,128)(2,1)}, u32[]{:S(2)}) copy-start(bf16[64,10922]{1,0:T(8,128)(2,1)} %in_ref.1) | copy-start | bytes 4194052
  7.2 24.6 %copy-start.13 = (bf16[64,5461]{1,0:T(8,128)(2,1)S(1)}, bf16[64,5461]{1,0:T(8,128)(2,1)}, u32[]{:S(2)}) copy-start(bf16[64,5461]{1,0:T(8,128)(2,1)} %out_ref.1) | copy-start | bytes 2097028
  7.2 33.1 %all-gather.6.cloned.1.call-start = ((), (), s32[]{:S(2)}) async-start(), calls=%async_computation.5 | async-start | bytes 1310720 | tf_op jit(solution)/shard_map/all_gather | solution.py:1207
  8.0 100.6 %all-gather.4.cloned.1.call-start = ((), (), s32[]{:S(2)}) async-start(), calls=%async_computation.4 | async-start | bytes 3932160 | tf_op jit(solution)/shard_map/all_gather | solution.py:1207
  30.3 181.7 %all-gather.8.cloned.1.call-start = ((), (), s32[]{:S(2)}) async-start(), calls=%async_computation.6 | async-start | bytes 7208960 | tf_op jit(solution)/shard_map/all_gather | solution.py:1207
  35.1 84.2 %copy-start.16 = (s32[8]{0:T(128)}, s32[8]{0:T(128)S(1)}, u32[]{:S(2)}) copy-start(s32[8]{0:T(128)S(1)} %get-tuple-element.143.prefix_ref) | copy-start | bytes 100
  105.3 326.3 %reduce-scatter.5.cloned.1.call-start = ((), (), s32[]{:S(2)}) async-start(), calls=%async_computation.7 | async-start | bytes 3604480 | tf_op jit(solution)/shard_map/reduce_scatter | solution.py:1249
  108.6 21.7 %copy-start.5 = (f32[8,2048]{1,0:T(8,128)}, f32[8,2048]{1,0:T(8,128)S(1)}, u32[]{:S(2)}) copy-start(f32[8,2048]{1,0:T(8,128)S(1)} %pad_convert_fusion.refs_2_.gains_ref) | copy-start | bytes 196612
  119.3 11.0 %copy-start.2 = (bf16[224,2048]{1,0:T(8,128)(2,1)S(1)}, bf16[224,2048]{1,0:T(8,128)(2,1)}, u32[]{:S(2)}) copy-start(bf16[224,2048]{1,0:T(8,128)(2,1)} %refs_3_.1) | copy-start | bytes 2752516
  119.3 11.0 %copy-start.10 = (bf16[256,2048]{1,0:T(8,128)(2,1)S(1)}, bf16[256,2048]{1,0:T(8,128)(2,1)}, u32[]{:S(2)}) copy-start(bf16[256,2048]{1,0:T(8,128)(2,1)} %all-gather.6.cloned.1.call-done.refs_1_) | copy-start | bytes 3145732
  315.3 160.7 %reduce-scatter.7.cloned.1.call-start = ((), (), s32[]{:S(2)}) async-start(), calls=%async_computation.8 | async-start | bytes 7208960 | tf_op jit(solution)/shard_map/reduce_scatter | solution.py:1210
  345.6 1.5 copy-start.4
  345.6 1.5 copy-start.6
  345.6 209.5 %reduce-scatter.9.cloned.1.call-start = ((), (), s32[]{:S(2)}) async-start(), calls=%async_computation.9 | async-start | bytes 3932160 | tf_op jit(solution)/shard_map/reduce_scatter | solution.py:1210
  452.8 23.6 %copy-start.1 = (bf16[1792,256]{1,0:T(8,128)(2,1)S(1)}, bf16[1792,256]{1,0:T(8,128)(2,1)}, u32[]{:S(2)}) copy-start(bf16[1792,256]{1,0:T(8,128)(2,1)} %get-tuple-element.84) | copy-start | bytes 2752516
  476.1 6.5 %copy-start.14 = (bf16[224,2048]{1,0:T(8,128)(2,1)S(1)}, bf16[224,2048]{1,0:T(8,128)(2,1)}, u32[]{:S(2)}) copy-start(bf16[224,2048]{1,0:T(8,128)(2,1)} %get-tuple-element.92) | copy-start | bytes 2752516
  476.1 93.5 %reduce-scatter.11.cloned.1.call-start = ((), (), s32[]{:S(2)}) async-start(), calls=%async_computation.10 | async-start | bytes 1310720 | tf_op jit(solution)/shard_map/reduce_scatter | solution.py:1210
  482.5 2.0 copy-start.15
  551.0 1.4 copy-start.8
  (5 other events, 5.5 us)
Sparse Core Ops, SparseCore 0:
  9.7 30.6 all-gather.5
  41.9 63.0 all-gather.3
  106.5 105.3 all-gather.7
  315.4 56.2 reduce-scatter.4
  373.9 102.0 reduce-scatter.6
  478.2 60.7 reduce-scatter.8
  541.9 27.6 reduce-scatter.10
